TPU v7x, 32 devices: a whole 2x2x4 slice. The times are simulated.
32 devices in a mesh: dp: 8 (over y, x, core), blk: 4 (over z).
Axes of the slice: x: 2, y: 2, z: 4, core: 2. Of those that a mesh axis runs over, the one named last changes fastest.
Arguments:
- tokens: bfloat16 [16, 16, 48, 768], P('dp', 'blk'), may hold values from -6 to 6
- frame_counts: int32 [16], P('dp'), may hold values from 4 to 16, as said below
- slot_mask: int32 [16, 16, 48], P('dp'), may hold values 0 or 1
- norm1_gain: float32 [768], replicated, may hold values from 0.5 to 1.5
- norm1_bias: float32 [768], replicated, may hold values from -2 to 2
- w_qkv: bfloat16 [768, 2304], replicated, may hold values from -0.21875 to 0.21875
- q_bias: float32 [768], replicated, may hold values from -2 to 2
- v_bias: float32 [768], replicated, may hold values from -2 to 2
- w_out: bfloat16 [768, 768], replicated, may hold values from -1.75 to 1.75
- out_bias: float32 [768], replicated, may hold values from -2 to 2
- norm2_gain: float32 [768], replicated, may hold values from 0.5 to 1.5
- norm2_bias: float32 [768], replicated, may hold values from -2 to 2
- w_up: bfloat16 [768, 3072], replicated, may hold values from -0.21875 to 0.21875
- up_bias: float32 [3072], replicated, may hold values from -2 to 2
- w_down: bfloat16 [3072, 768], replicated, may hold values from -0.109375 to 0.109375
- down_bias: float32 [768], replicated, may hold values from -2 to 2
- norm3_gain: float32 [768], replicated, may hold values from 0.5 to 1.5
- norm3_bias: float32 [768], replicated, may hold values from -2 to 2
- w_align: bfloat16 [768, 1024], replicated, may hold values from -0.21875 to 0.21875
- align_bias: float32 [1024], replicated, may hold values from -2 to 2
- cot_block: bfloat16 [16, 16, 48, 768], P('dp', 'blk'), may hold values from -6 to 6
- cot_align: bfloat16 [16, 16, 48, 1024], P('dp', 'blk'), may hold values from -6 to 6
Outputs:
- block_out: bfloat16 [16, 16, 48, 768], P('dp', 'blk')
- aligned: bfloat16 [16, 16, 48, 1024], P('dp', 'blk')
- grad_tokens: bfloat16 [16, 16, 48, 768], P('dp', 'blk')
- grad_norm1_gain: float32 [768], replicated
- grad_norm1_bias: float32 [768], replicated
- grad_w_qkv: float32 [768, 2304], P('dp')
- grad_q_bias: float32 [768], replicated
- grad_v_bias: float32 [768], replicated
- grad_w_out: float32 [768, 768], P('dp')
- grad_out_bias: float32 [768], replicated
- grad_norm2_gain: float32 [768], replicated
- grad_norm2_bias: float32 [768], replicated
- grad_w_up: float32 [768, 3072], P('dp')
- grad_up_bias: float32 [3072], replicated
- grad_w_down: float32 [3072, 768], P('dp')
- grad_down_bias: float32 [768], replicated
- grad_norm3_gain: float32 [768], replicated
- grad_norm3_bias: float32 [768], replicated
- grad_w_align: float32 [768, 1024], P('dp')
- grad_align_bias: float32 [1024], replicated
Inputs may be any that keep to these rules, and one draw needn't show every extreme that they name: `frame_counts`: each clip has 4, 8 or 16 real frames; in each aligned block of 2 clips (the clips of one index of dp) at least one has 16.
All inputs are finite; a program needn't handle non-finite values. No bound on the sum of `slot_mask` on one device may be relied on, other than what follows from the above.
Results may differ from a plain program's by a relative error of at most 0.013.
Values may be sent and summed in bfloat16 or wider, within the bound.
A program may use at most 192 MiB of HBM per device.

v0:
```python
import math

import jax
import jax.numpy as jnp
from jax import lax
from jax.experimental import pallas as pl
from jax.experimental.pallas import tpu as pltpu
from jax.sharding import PartitionSpec as P

HEADS = 12


EPSILON = 1e-06
SQRT_HALF = 0.7071067811865476
INV_ROOT_TAU = 0.3989422804014327
MESH = pl.DeviceIdType.MESH
GRID = (8, 4)


NT = (((1,), (1,)), ((), ()))
TN = (((0,), (0,)), ((), ()))
CHUNKS = 4


def dot(left, right, dims=(((1,), (0,)), ((), ()))):
    return lax.dot_general(left, right, dims, preferred_element_type=jnp.float32)


def remote_copy(src, dst, send, recv, device):
    return pltpu.make_async_remote_copy(
        src_ref=src, dst_ref=dst, send_sem=send, recv_sem=recv, device_id=device, device_id_type=MESH
    )


N1_GAIN, N1_BIAS, Q_BIAS, V_BIAS, OUT_BIAS, N2_GAIN, N2_BIAS, DOWN_BIAS, N3_GAIN, N3_BIAS, UP_BIAS, ALIGN_BIAS = (
    0, 1, 2, 3, 4, 5, 6, 7, 8, 9, 10, 14,
)
PACK_ROWS = 16
TILE = 512


def row_of(pack, row, start, size):
    width = pack.shape[1]
    parts = []
    while size > 0:
        line, column = row + start // width, start % width
        take = min(size, width - column)
        parts.append(pack[line : line + 1, column : column + take])
        start, size = start + take, size - take
    return parts[0] if len(parts) == 1 else jnp.concatenate(parts, axis=1)


def fill_pack(pack, rows, refs):
    width = pack.shape[1]
    for row, ref in zip(rows, refs):
        for start in range(0, ref.shape[0], width):
            size = min(width, ref.shape[0] - start)
            line = row + start // width
            pack[line : line + 1, 0:size] = ref[pl.ds(start, size)].reshape(1, size)


def norm_rows(values):
    center = values - jnp.mean(values, axis=-1, keepdims=True)
    inverse = lax.rsqrt(jnp.mean(center * center, axis=-1, keepdims=True) + EPSILON)
    return center * inverse, inverse


def put_visible(vis, visible_t, z):
    piece = vis.shape[0] // 2
    for c in range(2):
        where = pl.ds(pl.multiple_of(z * piece, piece), piece)
        vis[pl.ds(c * piece, piece), :] = visible_t[where, c : c + 1]


JOBS = (
    (4, 0, 96, 0, 1024, 2048),
    (3, 0, 96, 0, 768, 0),
    (3, 96, 96, 0, 768, 768),
    (3, 192, 96, 0, 768, 1536),
    (3, 288, 96, 0, 768, 2304),
    (2, 0, 96, 0, 768, 0),
    (2, 0, 96, 768, 768, 768),
    (2, 0, 96, 1536, 768, 1536),
    (2, 0, 96, 2304, 768, 2304),
    (1, 0, 96, 0, 768, 0),
    (0, 0, 96, 0, 384, 768),
    (0, 0, 96, 384, 384, 1152),
    (0, 0, 96, 768, 384, 1536),
)
COUNT = len(JOBS)
PLAIN = 10
KEY_BLOCK = 256
NORM_ROWS = 96
PLAN = (
    (0, "far"), (0, 0), "e3", "norm3", (0, "own"), (0, 1), (1, "far"), (1, 0), "feed", (1, "own"), (1, 1),
    (5, "far"), (5, 0), "e2", (0, 2), "norm2", (1, 2), "back_att", (5, "own"), (5, 1), (0, 3), (2, "far"), (2, 0),
    (2, "own"), (1, 3), (3, "far"), (3, 0), (3, "own"), (4, "far"), (4, 0), (2, 1), (6, "far"), (6, 0), (4, "own"),
    (5, 2), (6, "own"), "settle0", (3, 1), "pair", (2, 2), "pair", (5, 3), (4, 1), "pair", (3, 2), "settle1",
    (0, 4), (2, 3), "pair", (6, 1), "pair", (4, 2), (1, 4), (3, 3), "settle2", (5, 4), (0, 5), "pair", (6, 2),
    "pair", (2, 4), (4, 3), (1, 5), "pair", (6, 3), (0, 6), (3, 4), (5, 5), "pair", "dx0", (4, 4), (1, 6), (2, 5),
    (10, "far"), (10, 0), "dx1", "dx2", (11, "far"), (11, 0), (6, 4), (5, 6), (3, 5), (7, "far"), (7, 0),
    (9, "far"), (9, 0), (11, "own"), (7, "own"), "dx3", (2, 6), (4, 5), (10, "own"), (10, 1), (9, "own"),
    (8, "far"), (8, 0), "sums", "vec0", (11, 1), "fwd0", (8, "own"), (6, 5), (10, 2), (7, 1), (12, "far"), (12, 0),
    "vec1", (11, 2), (10, 3), "vec2", (9, 1), "fwd1", (3, 6), (7, 2), (11, 3), "vec3", (8, 1), (4, 6), "vec4",
    (9, 2), (7, 3), "vec5", (10, 4), (11, 4), (8, 2), "norm1", (9, 3), (12, "own"), (12, 1), (7, 4), (10, 5),
    (6, 6), (8, 3), (12, 2), (11, 5), (9, 4), (10, 6), (12, 3), (7, 5), (8, 4), (11, 6), (12, 4), (9, 5), (7, 6),
    (8, 5), (9, 6), (12, 5), (8, 6), (12, 6),
)


def add_into(target, first, second):
    lead = target.shape[:-2]

    def body(k, _):
        if len(lead) == 0:
            at = (pl.ds(pl.multiple_of(k * 16, 16), 16), slice(None))
        elif len(lead) == 1:
            at = (k,)
        else:
            at = (k // lead[1], lax.rem(k, lead[1]))
        target[at] = first[at] + second[at]
        return 0

    lax.fori_loop(0, math.prod(lead) if lead else target.shape[0] // 16, body, 0)


VIS, KEY, INV2, INV3, STATS = 0, 1, 2, 3, 8


def layer_kernel(*refs):
    slot_mask, counts, vectors_h, refs = refs[0], refs[1], refs[2:14], refs[14:]
    tok_h, cot_a_h, cot_b_h, w_align, w_down, w_up, w_out, w_qkv = refs[:8]
    block_out, align_out, grad_tokens, vec_out = refs[8:12]
    outs = refs[12:17]
    rest = refs[17:]
    own, got0, got1, got2 = (rest[i * COUNT : (i + 1) * COUNT] for i in range(4))
    rest = rest[4 * COUNT :]
    gotz, gotq = rest[:PLAIN], rest[PLAIN:COUNT]
    rest = rest[COUNT:]
    vec_got, vectors = rest[0], rest[1:13]
    (
        pack, side_v,
        align_v, down_v, up_v, out_v, low_v, tok, xall, n1, qkv, own_att, att, lse_rows, spread_rows,
        mid_v, e_v, normed, ring, slope, ld, l2, l3, la, unit2, unit3, cot_a, cot_b,
        grad_att, n1s, grad_q,
        load_sem, send0, recv0, send1, recv1, send2, recv2, sendz, recvz, sendq, recvq, out_sem, outq_sem, vsend, vrecv,
        tok_send, tok_recv, att_send, att_recv, in_send, in_recv,
        pair_send, pair_recv, end_send, end_recv, out_send, out_recv, put_sem, vector_sem,
    ) = rest[13:]

    dp = lax.axis_index("dp")
    z = lax.axis_index("blk")
    core = lax.rem(dp, 2)
    x = lax.rem(dp // 2, 2)
    y = dp // 4
    clip, side = z // 2, lax.rem(z, 2)
    to_core = (dp + 1 - 2 * core, z)
    to_x = (dp + 2 - 4 * x, z)
    to_y = (dp + 4 - 8 * y, z)
    partner = z + 1 - 2 * side
    to_z1 = (dp, partner)
    to_z2 = (dp, lax.rem(z + 2, 4))
    to_z3 = (dp, 3 - z)
    is_mid = (z == 1) | (z == 2)
    is_end = (z == 0) | (z == 3)
    near, far = 3 - z, lax.rem(z + 2, 4)
    other_mid = 2 - clip
    piece, width = tok.shape[1], tok.shape[2]
    rows, half, wide = 2 * piece, width // 2, up_v.shape[1]
    low = jnp.bfloat16
    low_d, low_o = n1.at[pl.ds(0, rows)], n1.at[pl.ds(rows, rows)]
    in_src = att
    from_end = [normed.at[pl.ds(k * piece, piece)] for k in range(2)]
    from_pair, total_in = (cot_b.at[pl.ds(k * piece, piece)] for k in range(2))

    def grad_at(m):
        return down_v.at[pl.ds((2 if m == 0 else 3) * width, width), pl.ds(half if m != 1 else 0, half)]

    def e_at(slot):
        return align_v.at[pl.ds(pl.multiple_of(slot * piece, piece), piece), pl.ds(0, width)]

    def slot_rows(slot):
        return pl.ds(pl.multiple_of(slot * piece, piece), piece)

    loads = {"tok": (tok_h, tok)}
    for m in range(3):
        column = pl.multiple_of(m * width + side * half, 128)
        loads["low%d" % m] = (w_qkv.at[:, pl.ds(column, half)], low_v.at[m])
    loads["out"] = (w_out, out_v)
    loads["up"] = (w_up, up_v)
    loads["down"] = (w_down, down_v)
    loads["cot_a"] = (cot_a_h, cot_a)
    loads["align"] = (w_align, align_v)
    loads["cot_b"] = (cot_b_h, cot_b)
    loads = {
        name: pltpu.make_async_copy(src, dst, load_sem.at[k]) for k, (name, (src, dst)) in enumerate(loads.items())
    }
    early = ("tok", "low0", "low1", "low2")
    for name in early:
        loads[name].start()
    small = [pltpu.make_async_copy(src, dst, vector_sem.at[k]) for k, (src, dst) in enumerate(zip(vectors_h, vectors))]
    for copy in small:
        copy.start()

    def ready(*names):
        for name in names:
            loads[name].wait()

    barrier = pltpu.get_barrier_semaphore()
    for device in (to_core, to_x, to_y, to_z1, to_z2, to_z3):
        pl.semaphore_signal(barrier, inc=1, device_id=device, device_id_type=MESH)
    pl.semaphore_wait(barrier, 6)
    step = piece // CHUNKS

    def tok_copy(kind, slot, k):
        at = pl.ds(k * step, step)
        source = xall.at[slot, at] if kind >= 2 else tok_h.at[1 - clip if kind == 0 else clip, at]
        device = (dp, other_mid) if kind == 0 else to_z1
        return remote_copy(source, xall.at[slot, at], tok_send.at[kind, k], tok_recv.at[slot, k], device)

    for k in range(CHUNKS):
        tok_copy(0, z, k).start()
    for k in range(CHUNKS):
        tok_copy(1, z, k).start()
    for copy in small:
        copy.wait()
    fill_pack(pack, VECTORS, vectors)
    vec_out[...] = jnp.zeros_like(vec_out)
    ready("tok")
    xall[z] = tok[clip]
    e_v[0:128, :] = jnp.zeros((128, width), jnp.float32)
    for c in range(2):
        e_v[c : c + 1, :] = jnp.concatenate(
            [
                jnp.where((slot_mask[c, f : f + 1, :] > 0) & (f < counts[c]), 1.0, 0.0)
                for f in range(slot_mask.shape[1])
            ],
            axis=1,
        )
    grad_q[...] = e_v[0:128, :].T
    for c in range(2):
        side_v[pl.ds(c * piece, piece), VIS : VIS + 1] = grad_q[pl.ds(pl.multiple_of(z * piece, piece), piece), c : c + 1]
    seen = jnp.where(clip == 0, grad_q[:, 0:1], grad_q[:, 1:2])
    side_v[:, KEY : KEY + 1] = jnp.where(seen > 0.0, 0.0, -1e30)
    row_bias = jnp.where(jnp.where(clip == 0, e_v[0:1, :], e_v[1:2, :]) > 0.0, 0.0, -1e30)
    columns = pl.ds(pl.multiple_of(side * half, 128), half)
    ready("low0", "low1", "low2")

    def project(slot):
        where = slot_rows(slot)

        def body(k, _):
            one, _ = norm_rows(xall[slot, pl.ds(pl.multiple_of(k * 96, 96), 96), :].astype(jnp.float32))
            at = pl.ds(pl.multiple_of(slot * piece + k * 96, 96), 96)
            n1[at, :] = (one * pack[N1_GAIN : N1_GAIN + 1, :] + pack[N1_BIAS : N1_BIAS + 1, :]).astype(low)
            return 0

        lax.fori_loop(0, piece // 96, body, 0)
        left = n1[where, :]
        qkv[0, where, :] = (dot(left, low_v[0]) + pack[Q_BIAS : Q_BIAS + 1, columns]).astype(low) * low(0.125)
        qkv[1, where, :] = dot(left, low_v[1]).astype(low)
        qkv[2, where, :] = (dot(left, low_v[2]) + pack[V_BIAS : V_BIAS + 1, columns]).astype(low)

    def tokens_of(number, _):
        first, second = jnp.where(is_mid, near, far), jnp.where(is_mid, far, near)
        slot = jnp.where(
            number == 0, z, jnp.where(number == 1, partner, jnp.where(number == 2, first, second))
        )

        @pl.when(number == 1)
        def _():
            for name in loads:
                if name not in early:
                    loads[name].start()

        @pl.when(is_mid & (number == 1))
        def _():
            for which, source in enumerate((near, far)):
                for k in range(CHUNKS):
                    tok_copy(1, source, k).wait_recv()
                    tok_copy(2 + which, source, k).start()
            for k in range(CHUNKS):
                tok_copy(1, partner, k).wait_recv()

        @pl.when(is_end & (number > 0))
        def _():
            for k in range(CHUNKS):
                tok_copy(1, slot, k).wait_recv()

        project(slot)
        return 0

    lax.fori_loop(0, 4, tokens_of, 0)
    lane = lax.broadcasted_iota(jnp.int32, (1, 128), 1)
    low_lane = lane < 64

    def att_copy(slot):
        return remote_copy(
            own_att.at[slot_rows(slot)], att.at[clip, side], att_send.at[slot], att_recv.at[z], (dp, slot)
        )

    def attend(number, _):
        slot = jnp.where(number == 0, far, jnp.where(number == 1, near, jnp.where(number == 2, partner, z)))
        where = slot_rows(slot)
        stats = jnp.zeros((piece, 128), jnp.float32)
        for t in range(half // 128):
            at = pl.ds(t * 128, 128)
            queries = qkv[0, where, at]
            keys = qkv[1, :, at]
            values = qkv[2, :, at]
            parts = []
            for a in range(2):
                mine = low_lane if a == 0 else jnp.logical_not(low_lane)
                masked = jnp.where(mine, queries, jnp.zeros_like(queries))
                scores = dot(masked, keys, NT) + row_bias
                top = jnp.max(scores, axis=-1, keepdims=True)
                expo = jnp.exp(scores - top)
                denominator = jnp.sum(expo, axis=-1, keepdims=True)
                parts.append(dot(expo.astype(low), values) * (1.0 / denominator))
                stats = jnp.where(lane == STATS + 2 * t + a, top + jnp.log(denominator), stats)
            own_att[where, at] = jnp.where(low_lane, parts[0], parts[1]).astype(low)
        side_v[where, STATS : STATS + 8] = stats[:, STATS : STATS + 8]

        @pl.when(number < 3)
        def _():
            att_copy(slot).start()

        return 0

    lax.fori_loop(0, 4, attend, 0)
    att[clip, side] = own_att[slot_rows(z), :]

    def tiles(count, size, body):
        def one_tile(t, _):
            body(t, pl.ds(pl.multiple_of(t * size, size), size))
            return 0

        lax.fori_loop(0, count, one_tile, 0)

    def chunks(body, carry, size=48):
        def one_chunk(k, carry):
            return body(pl.ds(pl.multiple_of(k * size, size), size), k, carry)

        return lax.fori_loop(0, rows // size, one_chunk, carry)

    def put_vector(row, start, value):
        at = 0
        while at < value.shape[1]:
            line, column = row + (start + at) // width, (start + at) % width
            take = min(value.shape[1] - at, width - column)
            vec_out[line : line + 1, column : column + take] = value[:, at : at + take]
            at += take

    def total(value):
        return jnp.sum(value.astype(jnp.float32), axis=0, keepdims=True)

    zero_row = jnp.zeros((1, width), jnp.float32)
    ready("cot_a")

    def mask(at, k, carry):
        value = (side_v[at, VIS : VIS + 1] * cot_a[at, :].astype(jnp.float32)).astype(low)
        cot_a[at, :] = value
        return carry + total(value)

    put_vector(ALIGN_BIAS, 0, chunks(mask, jnp.zeros((1, cot_a.shape[1]), jnp.float32)))
    lse_rows[...] = side_v[...].T[STATS : STATS + 8]

    def shares_of(source, target, count):
        for c in range(0, source.shape[1], 128):
            flipped = source[:, pl.ds(c, 128)].T
            at = 0
            while at < 128:
                share, inside = (c + at) // count, (c + at) % count
                take = min(128 - at, count - inside)
                rel = jnp.where(core == share % 2, 1, 0)
                target[rel, share // 2, pl.ds(inside, take), :] = flipped[at : at + take]
                at += take

    shares_of(n1, n1s, width // 8)

    def settle_att(number, _):
        slot = lax.rem(z + number, 4)
        att_copy(slot).wait_send()
        remote_copy(
            own_att.at[slot_rows(slot)], att.at[slot // 2, lax.rem(slot, 2)],
            att_send.at[slot], att_recv.at[slot], (dp, slot),
        ).wait_recv()
        return 0

    lax.fori_loop(1, 4, settle_att, 0)
    for k in range(CHUNKS):
        tok_copy(0, z, k).wait_send()
        tok_copy(1, z, k).wait_send()

    @pl.when(is_mid)
    def _():
        for k in range(CHUNKS):
            for which, slot in enumerate((near, far)):
                tok_copy(2 + which, slot, k).wait_send()

    for c in range(2):
        for h in range(2):
            normed[pl.ds(c * piece, piece), pl.ds(h * half, half)] = att[c, h]
    shares_of(normed, la, width // 8)
    ready("out")

    def mix(t, at):
        mixed = dot(normed[...], out_v[:, at]) + pack[OUT_BIAS : OUT_BIAS + 1, at]
        mid_v[pl.ds(0, piece), at] = tok[0, :, at].astype(jnp.float32) + mixed[:piece]
        mid_v[pl.ds(piece, piece), at] = tok[1, :, at].astype(jnp.float32) + mixed[piece:]

    tiles(3, 256, mix)

    def norm(gain, bias, unit, inv):
        def body(at, k, _):
            one, inverse = norm_rows(mid_v[at, :])
            unit[at, :] = one.astype(low)
            side_v[at, inv : inv + 1] = inverse
            normed[at, :] = (one * pack[gain : gain + 1, :] + pack[bias : bias + 1, :]).astype(low)
            return 0

        chunks(body, 0, NORM_ROWS)

    norm(N2_GAIN, N2_BIAS, unit2, INV2)
    shares_of(normed, l2, width // 8)
    ready("up")

    def up(t, at):
        e_v[...] = dot(normed[...], up_v[:, at]) + pack[pl.ds(UP_BIAS + t, 1), :]

        def gelu(here, k, _):
            values = e_v[here, :]
            cdf = 0.5 * (1.0 + lax.erf(values * SQRT_HALF))
            ring[k, :, at] = (values * cdf).astype(low)
            slope[here, at] = (cdf + values * jnp.exp(-0.5 * values * values) * INV_ROOT_TAU).astype(low)
            return 0

        chunks(gelu, 0)
        for c in range(0, width, 128):
            rel = core if c < half else 1 - core
            columns_at = pl.ds(pl.multiple_of(t * width + c, 128), 128)
            ld[1 - rel, t, pl.ds(c % half, 128), :] = ring[:, :, columns_at].reshape(rows, 128).T

    tiles(4, width, up)
    ready("down")

    def down(t, at):
        mid_v[:, at] = (
            mid_v[:, at] + dot(ring[...].reshape(rows, wide), down_v[:, at]) + pack[DOWN_BIAS : DOWN_BIAS + 1, at]
        )

    tiles(3, 256, down)

    def staged(j, target):
        return pltpu.make_async_copy(own[j], target, put_sem.at[j])

    def put_block(at, k, _):
        own[1][k // 4, lax.rem(k, 4)] = (side_v[at, VIS : VIS + 1] * mid_v[at, :]).astype(low)
        return 0

    chunks(put_block, 0)
    staged(1, block_out).start()
    norm(N3_GAIN, N3_BIAS, unit3, INV3)
    shares_of(normed, l3, width // 8)
    ready("align", "cot_b")

    def head(t, at):
        bias = pack[pl.ds(ALIGN_BIAS + t // 3, 1), pl.ds(pl.multiple_of(lax.rem(t, 3) * 256, 256), 256)]
        value = dot(normed[...], align_v[:, at]) + bias
        value = (side_v[pl.ds(0, rows), VIS : VIS + 1] * value).astype(low)
        for k in range(8):
            own[0][k // 4, k % 4, :, at] = value[k * 48 : (k + 1) * 48]

    tiles(4, 256, head)
    staged(0, align_out).start()

    def buffer_of(j):
        return ring.at[:, :, pl.ds(JOBS[j][5], JOBS[j][4])]

    def copies0(j):
        for h in range(2):
            yield remote_copy(
                buffer_of(j).at[pl.ds(4 * h, 4)], got0[j].at[h], send0.at[j, h], recv0.at[j, h], to_core
            )

    def copies1(j):
        yield remote_copy(
            own[j].at[0, pl.ds(2 * (1 - x), 2)], got1[j].at[0], send1.at[j, 0], recv1.at[j, 0], to_x
        )
        yield remote_copy(
            own[j].at[1, pl.ds(2 * (1 - y), 2)], got1[j].at[1], send1.at[j, 1], recv1.at[j, 1], to_y
        )

    def copies2(j):
        yield remote_copy(own[j].at[0, 2 * x + 1 - y], got2[j].at[0], send2.at[j, 0], recv2.at[j, 0], to_y)
        yield remote_copy(own[j].at[1, 2 * y + 1 - x], got2[j].at[1], send2.at[j, 1], recv2.at[j, 1], to_x)

    def shares(j):
        return (own[j].at[0, 2 * x + y], own[j].at[1, 2 * y + x])

    def copiesz(j, slot, device):
        for h, share in enumerate(shares(j)):
            yield remote_copy(share, gotz[j].at[slot, h], sendz.at[j, slot, h], recvz.at[j, slot, h], device)

    def copiesq(j, source, slot, device):
        got, m = gotq[j - PLAIN], j - PLAIN
        for h, share in enumerate(shares(j)):
            yield remote_copy(
                share if source is None else got.at[source, h],
                got.at[slot, h], sendq.at[m, slot, h], recvq.at[m, slot, h], device,
            )

    def result(j, h, source):
        matrix, row, count, column, size, _ = JOBS[j]
        return pltpu.make_async_copy(
            source, outs[matrix].at[pl.ds(row + h * count // 2, count // 2), pl.ds(column, size)], out_sem.at[j, h]
        )

    def result_q(j, h, which, source):
        count, m = JOBS[j][2] // 2, j - PLAIN
        at = side if which == 0 else 1 - side
        column = pl.multiple_of(m * width + at * half, 128)
        return pltpu.make_async_copy(
            source, outs[0].at[pl.ds(h * count, count), pl.ds(column, half)], outq_sem.at[m, which, h]
        )

    def stage(j, number):
        if number == 0:
            for copy in copies0(j):
                copy.start()
        if number == 1:
            for copy in copies0(j):
                copy.wait()
            add_into(own[j], own[j], got0[j])
            for copy in copies1(j):
                copy.start()
        if number == 2:
            for copy in copies1(j):
                copy.wait()
            first, second = (own[j].at[0, pl.ds(2 * x, 2)], own[j].at[1, pl.ds(2 * y, 2)])
            add_into(first, first, got1[j].at[0])
            add_into(second, second, got1[j].at[1])
            for copy in copies2(j):
                copy.start()
        if number == 3:
            for copy in copies2(j):
                copy.wait()
            for h, share in enumerate(shares(j)):
                add_into(share, share, got2[j].at[h])

            @pl.when(is_end)
            def _():
                for copy in copiesq(j, None, 0, to_z1) if j >= PLAIN else copiesz(j, 0, to_z1):
                    copy.start()

        if number >= 4 and j >= PLAIN:
            stage_q(j, number)
            return
        if number == 4:

            @pl.when(is_mid)
            def _():
                for copy in copiesz(j, 0, to_z1):
                    copy.wait_recv()
                for h, share in enumerate(shares(j)):
                    add_into(share, share, gotz[j].at[0, h])
                for copy in copiesz(j, 1, to_z3):
                    copy.start()

            @pl.when(is_end)
            def _():
                for copy in copiesz(j, 0, to_z1):
                    copy.wait_send()

        if number == 5:

            @pl.when(is_mid)
            def _():
                for copy in copiesz(j, 1, to_z3):
                    copy.wait()
                for h, share in enumerate(shares(j)):
                    add_into(share, share, gotz[j].at[1, h])
                for copy in copiesz(j, 0, to_z1):
                    copy.start()
                for h, share in enumerate(shares(j)):
                    result(j, h, share).start()

        if number == 6:

            @pl.when(is_mid)
            def _():
                for copy in copiesz(j, 0, to_z1):
                    copy.wait_send()

            @pl.when(is_end)
            def _():
                for copy in copiesz(j, 0, to_z1):
                    copy.wait_recv()
                for h in range(2):
                    result(j, h, gotz[j].at[0, h]).start()

    def stage_q(j, number):
        got = gotq[j - PLAIN]
        if number == 4:

            @pl.when(is_mid)
            def _():
                for copy in copiesq(j, None, 1, to_z3):
                    copy.start()
                for copy in copiesq(j, None, 0, to_z1):
                    copy.wait_recv()
                for copy in copiesq(j, 0, 2, to_z3):
                    copy.start()

            @pl.when(is_end)
            def _():
                for copy in copiesq(j, None, 0, to_z1):
                    copy.wait_send()

        if number == 5:

            @pl.when(is_mid)
            def _():
                for copy in copiesq(j, None, 1, to_z3):
                    copy.wait()
                for copy in copiesq(j, 0, 2, to_z3):
                    copy.wait()
                for h, share in enumerate(shares(j)):
                    add_into(share, share, got.at[2, h])
                    add_into(got.at[0, h], got.at[0, h], got.at[1, h])
                for copy in copiesq(j, None, 1, to_z1):
                    copy.start()
                for copy in copiesq(j, 0, 0, to_z1):
                    copy.start()
                for h, share in enumerate(shares(j)):
                    result_q(j, h, 0, share).start()
                    result_q(j, h, 1, got.at[0, h]).start()

        if number == 6:

            @pl.when(is_mid)
            def _():
                for copy in copiesq(j, None, 1, to_z1):
                    copy.wait_send()
                for copy in copiesq(j, 0, 0, to_z1):
                    copy.wait_send()

            @pl.when(is_end)
            def _():
                for copy in copiesq(j, None, 1, to_z1):
                    copy.wait_recv()
                for copy in copiesq(j, 0, 0, to_z1):
                    copy.wait_recv()
                for h in range(2):
                    result_q(j, h, 0, got.at[0, h]).start()
                    result_q(j, h, 1, got.at[1, h]).start()

    def results_done():
        for j in range(COUNT):
            for h in range(2):
                if j < PLAIN:
                    result(j, h, gotz[j].at[0, h]).wait()
                else:
                    for which in range(2):
                        result_q(j, h, which, gotq[j - PLAIN].at[0, h]).wait()

    def gradient(j, mine, left, right):
        count, size = JOBS[j][2], JOBS[j][4]
        target = own[j] if mine else buffer_of(j)
        for c in range(0, size, min(size, 384 if size % 384 == 0 else 512)):
            at = pl.ds(c, min(size, 384 if size % 384 == 0 else 512))
            value = dot(left, right(at)).astype(low)
            for chip in range(4):
                cy, cx = chip // 2, chip % 2
                for h in range(2):
                    k = 2 * cx + cy if h == 0 else 2 * cy + cx
                    start = chip * count + h * count // 2
                    part = value[start : start + count // 2]
                    if mine:
                        target[h, k, :, at] = part
                    else:
                        target[4 * h + k, :, at] = part

    def job(j, mine):
        matrix, row, count, column, size, _ = JOBS[j]
        lhs, rhs = ((n1s, None), (la, low_o), (l2, slope), (ld, low_d), (l3, cot_a))[matrix]
        left = lhs[1 if mine else 0, :, pl.ds(row, count), :].reshape(4 * count, lhs.shape[3])
        if matrix == 0:
            gradient(j, mine, left, lambda at: grad_at(j - PLAIN)[...])
        else:
            gradient(j, mine, left, lambda at: rhs[:, pl.ds(column + at.start, at.size)])

    def norm_back(e, one, inverse, gain):
        scaled = e * gain
        return inverse * (
            scaled
            - jnp.mean(scaled, axis=-1, keepdims=True)
            - one * jnp.mean(scaled * one, axis=-1, keepdims=True)
        )

    def norm_pass(unit, inv, gain_row, base, low_target, sums):
        def body(at, k, carry):
            e = e_v[at, :]
            one = unit[at, :].astype(jnp.float32)
            value = base(at) + norm_back(e, one, side_v[at, inv : inv + 1], pack[gain_row : gain_row + 1, :])
            mid_v[at, :] = value
            rounded = value.astype(low)
            low_target[at, :] = rounded
            return (carry[0] + total(e * one), carry[1] + total(e), carry[2] + total(rounded))

        for row, value in zip(sums, chunks(body, (zero_row,) * 3, NORM_ROWS)):
            put_vector(row, 0, value)

    def e3():
        def body(t, at):
            e_v[:, at] = dot(cot_a[...], align_v[at, :], NT)

        tiles(3, 256, body)

    def norm3():
        norm_pass(
            unit3, INV3, N3_GAIN, lambda at: side_v[at, VIS : VIS + 1] * cot_b[at, :].astype(jnp.float32), low_d,
            (N3_GAIN, N3_BIAS, DOWN_BIAS),
        )

    def feed():
        def body(t, at):
            value = (dot(low_d[...], down_v[at, :], NT) * slope[:, at].astype(jnp.float32)).astype(low)
            slope[:, at] = value
            vec_out[pl.ds(UP_BIAS + t, 1), :] = total(value)

        tiles(4, width, body)

    def e2():
        def body(t, at):
            e_v[:, at] = dot(slope[...], up_v[at, :], NT)

        tiles(3, 256, body)

    def norm2():
        norm_pass(unit2, INV2, N2_GAIN, lambda at: mid_v[at, :], low_o, (N2_GAIN, N2_BIAS, OUT_BIAS))

    def in_copy(slot, t):
        at = pl.ds(t * 128, 128)
        return remote_copy(
            in_src.at[slot // 2, lax.rem(slot, 2), :, at], grad_att.at[z, :, at],
            in_send.at[slot, t], in_recv.at[z, t], (dp, slot),
        )

    def back_att():
        for h in range(2):
            value = dot(low_o[...], out_v[pl.ds(h * half, half), :], NT).astype(low)
            for c in range(2):
                in_src[c, h] = value[c * piece : (c + 1) * piece]
        for t in range(half // 128):

            def start(number, _):
                in_copy(lax.rem(z + number, 4), t).start()
                return 0

            lax.fori_loop(1, 4, start, 0)
        grad_att[z] = in_src[clip, side]

    def settle(t):
        at = pl.ds(t * 128, 128)

        def body(number, _):
            slot = lax.rem(z + number, 4)
            in_copy(slot, t).wait_send()
            remote_copy(
                in_src.at[0, 0, :, at], grad_att.at[slot, :, at], in_send.at[slot, t], in_recv.at[slot, t], (dp, slot)
            ).wait_recv()
            return 0

        lax.fori_loop(1, 4, body, 0)

        def spread(slot, _):
            where = slot_rows(slot)
            stats = jnp.zeros((piece, 128), jnp.float32)
            product = grad_att[slot, :, at].astype(jnp.float32) * own_att[where, at].astype(jnp.float32)
            for a in range(2):
                mine = low_lane if a == 0 else jnp.logical_not(low_lane)
                value = jnp.sum(jnp.where(mine, product, 0.0), axis=-1, keepdims=True)
                stats = jnp.where(lane == STATS + a, value, stats)
            side_v[where, STATS : STATS + 2] = stats[:, STATS : STATS + 2]
            return 0

        lax.fori_loop(0, 4, spread, 0)
        spread_rows[2 * t : 2 * t + 2, :] = side_v[...].T[STATS : STATS + 2]

    def pair(number):
        t, b = number // 3, lax.rem(number, 3)
        at = pl.ds(pl.multiple_of(t * 128, 128), 128)
        queries = qkv[0, :, at]
        grads = grad_att[:, :, at].reshape(4 * piece, 128)
        keys_at = pl.ds(pl.multiple_of(b * KEY_BLOCK, KEY_BLOCK), KEY_BLOCK)
        keys = qkv[1, keys_at, at]
        values = qkv[2, keys_at, at]
        grad_k = jnp.zeros((KEY_BLOCK, 128), jnp.float32)
        grad_v = jnp.zeros((KEY_BLOCK, 128), jnp.float32)
        grad_queries = jnp.where(b == 0, 0.0, grad_q[...])
        for a in range(2):
            mine = low_lane if a == 0 else jnp.logical_not(low_lane)
            zero = jnp.zeros((), low)
            q_mine = jnp.where(mine, queries, zero)
            g_mine = jnp.where(mine, grads, zero)
            k_mine = jnp.where(mine, keys, zero)
            row = pl.ds(2 * t + a, 1)
            scores = dot(keys, q_mine, NT) + side_v[keys_at, KEY : KEY + 1]
            probs = jnp.exp(scores - lse_rows[row, :])
            back = (probs * (dot(values, g_mine, NT) - spread_rows[row, :])).astype(low)
            grad_v = grad_v + dot(probs.astype(low), g_mine)
            grad_k = grad_k + dot(back, q_mine)
            grad_queries = grad_queries + dot(back, k_mine, TN)
        grad_at(1)[keys_at, at] = grad_k.astype(low)
        grad_at(2)[keys_at, at] = grad_v.astype(low)
        grad_q[...] = grad_queries

        @pl.when(b == 2)
        def _():
            grad_at(0)[:, at] = (grad_q[...] * 0.125).astype(low)

    def pair_copy():
        return remote_copy(e_at(partner), from_pair, pair_send, pair_recv, to_z1)

    def end_copy(which, slot):
        return remote_copy(e_at(slot), from_end[which], end_send.at[which], end_recv.at[which], to_z1)

    def out_copy(which, slot):
        return remote_copy(e_at(slot), total_in, out_send.at[which], out_recv, (dp, slot))

    targets = (3 - 3 * clip, 2 - clip)
    mine_rows = slot_rows(clip)

    def dx(number):
        slot = (targets + (partner, z))[number]
        where = slot_rows(slot)
        value = sum(dot(grad_at(m)[where, :], low_v[m], NT) for m in range(3))
        e_at(slot)[...] = value.astype(low)
        if number == 3:
            e_v[mine_rows, :] = value
        if number < 2:

            @pl.when(is_end)
            def _():
                end_copy(number, slot).start()

        if number == 2:
            pair_copy().start()
        one, _ = norm_rows(xall[slot].astype(jnp.float32))
        for row, term in ((N1_GAIN, total(value * one)), (N1_BIAS, total(value))):
            vec_out[row : row + 1, :] = vec_out[row : row + 1, :] + term

    def sums():
        spot = lax.broadcasted_iota(jnp.int32, (1, width), 1)
        for row, m in ((Q_BIAS, 0), (V_BIAS, 2)):
            value = total(grad_at(m)[...])
            value = jnp.concatenate([value, value], axis=1)
            put_vector(row, 0, jnp.where((spot < half) == (side == 0), value, 0.0))

    def forward(which):
        @pl.when(is_mid)
        def _():
            slot = targets[which]
            end_copy(which, slot).wait_recv()
            add_into(e_at(slot), e_at(slot), from_end[which])
            out_copy(which, slot).start()

    vec_devices = (to_core, to_x, to_y, to_z1, to_z2)

    def vec_copy(k):
        return remote_copy(vec_out, vec_got.at[k], vsend.at[k], vrecv.at[k], vec_devices[k])

    def vec(k):
        if k > 0:
            vec_copy(k - 1).wait()
            vec_out[...] = vec_out[...] + vec_got[k - 1]
        if k < 5:
            vec_copy(k).start()

    def norm1():
        pair_copy().wait()
        e_v[mine_rows, :] = e_v[mine_rows, :] + from_pair[...].astype(jnp.float32)
        out_copy(0, partner).wait_recv()
        e_v[slot_rows(1 - clip), :] = total_in[...].astype(jnp.float32)

        def body(at, k, _):
            half_clip = pl.ds(pl.multiple_of(lax.rem(k, 2) * NORM_ROWS, NORM_ROWS), NORM_ROWS)
            one, inverse = norm_rows(tok[k // 2, half_clip, :].astype(jnp.float32))
            value = mid_v[at, :] + norm_back(e_v[at, :], one, inverse, pack[N1_GAIN : N1_GAIN + 1, :])
            low_d[at, :] = value.astype(low)
            return 0

        chunks(body, 0, NORM_ROWS)
        pltpu.make_async_copy(low_d, grad_tokens, put_sem.at[2]).start()

    singles = dict(
        e3=e3, norm3=norm3, feed=feed, e2=e2, norm2=norm2, back_att=back_att, sums=sums, norm1=norm1
    )
    several = dict(settle=settle, dx=dx, fwd=forward, vec=vec)
    staged(0, align_out).wait()
    staged(1, block_out).wait()

    def run(entries):
        for entry in entries:
            if isinstance(entry, tuple):
                if entry[1] in ("far", "own"):
                    job(entry[0], entry[1] == "own")
                else:
                    stage(*entry)
            elif entry in singles:
                singles[entry]()
            else:
                several[entry[:-1]](int(entry[-1]))

    spots = [k for k, entry in enumerate(PLAN) if entry == "pair"]
    run(PLAN[: spots[0]])

    def pair_and_more(number, _):
        pair(number)
        for k in range(len(spots) - 1):
            if spots[k] + 1 < spots[k + 1]:

                @pl.when(number == k)
                def _():
                    run(PLAN[spots[k] + 1 : spots[k + 1]])

        return 0

    lax.fori_loop(0, len(spots), pair_and_more, 0)
    run(PLAN[spots[-1] + 1 :])
    results_done()
    pltpu.make_async_copy(low_d, grad_tokens, put_sem.at[2]).wait()

    @pl.when(is_mid)
    def _():
        for which in range(2):
            out_copy(which, targets[which]).wait_send()

    @pl.when(is_end)
    def _():
        for which in range(2):
            end_copy(which, targets[which]).wait_send()


def layer(slot_mask, counts, vectors, tok, cot_a, cot_b, w_align, w_down, w_up, w_out, w_qkv):
    _, piece, width = tok.shape
    rows, half, wide, align = 2 * piece, width // 2, w_up.shape[1], w_align.shape[1]
    low, full = jnp.bfloat16, jnp.float32
    vmem = pl.BlockSpec(memory_space=pltpu.VMEM)
    hbm = pl.BlockSpec(memory_space=pl.ANY)
    dma = pltpu.SemaphoreType.DMA
    v = pltpu.VMEM
    shapes = [(2, 4, job[2] // 2, job[4]) for job in JOBS]
    scratch = (
        [v(shape, low) for shape in shapes]
        + [v(shape, low) for shape in shapes]
        + [v((2, 2) + shape[2:], low) for shape in shapes]
        + [v((2,) + shape[2:], low) for shape in shapes]
        + [v((2, 2) + shape[2:], low) for shape in shapes[:PLAIN]]
        + [v((3, 2) + shape[2:], low) for shape in shapes[PLAIN:]]
        + [v((5, PACK_ROWS, width), full)]
        + [v(vector.shape, full) for vector in vectors]
        + [v((PACK_ROWS, width), full), v((4 * piece, 128), full)]
        + [v(w_align.shape, low), v(w_down.shape, low), v(w_up.shape, low), v(w_out.shape, low)]
        + [v((3, width, half), low), v((2, piece, width), low), v((4, piece, width), low), v((4 * piece, width), low)]
        + [v((3, 4 * piece, half), low), v((4 * piece, half), low), v((2, 2, piece, half), low)]
        + [v((8, 4 * piece), full)] * 2
        + [v((rows, width), full), v((rows, width), full), v((rows, width), low), v((8, 48, wide), low)]
        + [v((rows, wide), low), v((2, 4, wide // 8, rows), low)]
        + [v((2, 4, width // 8, rows), low)] * 3
        + [v((rows, width), low)] * 2
        + [v((rows, align), low), v((rows, width), low)]
        + [v((4, piece, half), low), v((2, 4, width // 8, 4 * piece), low), v((4 * piece, 128), full)]
        + [dma((10,))]
        + [dma((COUNT, 2))] * 6
        + [dma((PLAIN, 2, 2))] * 2
        + [dma((3, 3, 2))] * 2
        + [dma((PLAIN, 2)), dma((3, 2, 2))]
        + [dma((5,))] * 2
        + [dma((4, CHUNKS))] * 2
        + [dma((4,))] * 2
        + [dma((4, 3))] * 2
        + [dma(())] * 2
        + [dma((2,))] * 2
        + [dma((2,)), dma(())]
        + [dma((3,)), dma((12,))]
    )
    struct = jax.ShapeDtypeStruct
    return pl.pallas_call(
        layer_kernel,
        name="layer",
        out_shape=[
            struct((2, 4, 48, width), low),
            struct((2, 4, 48, align), low),
            struct((rows, width), low),
            struct((PACK_ROWS, width), full),
        ]
        + [struct((w.shape[0] // 8, w.shape[1]), low) for w in (w_qkv, w_out, w_up, w_down, w_align)],
        in_specs=[vmem, pl.BlockSpec(memory_space=pltpu.SMEM)] + [hbm] * 20,
        out_specs=[hbm, hbm, hbm, vmem] + [hbm] * 5,
        scratch_shapes=scratch,
        compiler_params=pltpu.CompilerParams(
            collective_id=0, has_side_effects=True, vmem_limit_bytes=63 * 2**20
        ),
    )(slot_mask, counts, *vectors, tok, cot_a, cot_b, w_align, w_down, w_up, w_out, w_qkv)


VECTORS = (
    N1_GAIN, N1_BIAS, Q_BIAS, V_BIAS, OUT_BIAS, N2_GAIN, N2_BIAS, DOWN_BIAS, N3_GAIN, N3_BIAS, UP_BIAS, ALIGN_BIAS,
)


def finish_kernel(*refs):
    shares, pack, through_in = refs[:5], refs[5], refs[6:9]
    wide, vectors, through_out = refs[9:14], refs[14:26], refs[26:29]
    low_v, wide_v, held, pack_v, vectors_v = refs[29:34], refs[34:39], refs[39:42], refs[42], refs[43:55]
    in_sem, out_sem, vector_sem = refs[55:]
    ins = [pltpu.make_async_copy(shares[k], low_v[k], in_sem.at[k]) for k in range(5)]
    outs = [pltpu.make_async_copy(wide_v[k], wide[k], out_sem.at[k]) for k in range(5)]
    through = [
        (
            pltpu.make_async_copy(through_in[k], held[k], in_sem.at[5 + k]),
            pltpu.make_async_copy(held[k], through_out[k], out_sem.at[5 + k]),
        )
        for k in range(3)
    ]
    pack_in = pltpu.make_async_copy(pack, pack_v, in_sem.at[8])
    for copy in [pack_in] + ins:
        copy.start()
    for copy, _ in through:
        copy.start()
    width = pack.shape[1]
    vectors_out = [
        pltpu.make_async_copy(vectors_v[k], vectors[k], vector_sem.at[k]) for k in range(len(vectors))
    ]
    pack_in.wait()
    for row, ref in zip(VECTORS, vectors_v):
        for start in range(0, ref.shape[0], width):
            size = min(width, ref.shape[0] - start)
            line = row + start // width
            ref[pl.ds(start, size)] = pack_v[line : line + 1, 0:size].reshape(size)
    for copy in vectors_out:
        copy.start()
    for k in range(5):
        ins[k].wait()
        wide_v[k][...] = low_v[k][...].astype(jnp.float32)
        outs[k].start()
    for first, second in through:
        first.wait()
        second.start()
    for copy in outs + vectors_out:
        copy.wait()
    for _, copy in through:
        copy.wait()


def finish(shares, pack, through, sizes):
    hbm = pl.BlockSpec(memory_space=pl.ANY)
    struct = jax.ShapeDtypeStruct
    results = pl.pallas_call(
        finish_kernel,
        name="finish",
        out_shape=[struct(share.shape, jnp.float32) for share in shares]
        + [struct((size,), jnp.float32) for size in sizes]
        + [struct(array.shape, array.dtype) for array in through],
        in_specs=[hbm] * 9,
        out_specs=[hbm] * 20,
        scratch_shapes=[pltpu.VMEM(share.shape, share.dtype) for share in shares]
        + [pltpu.VMEM(share.shape, jnp.float32) for share in shares]
        + [pltpu.VMEM(array.shape, array.dtype) for array in through]
        + [pltpu.VMEM(pack.shape, pack.dtype)]
        + [pltpu.VMEM((size,), jnp.float32) for size in sizes]
        + [pltpu.SemaphoreType.DMA((9,)), pltpu.SemaphoreType.DMA((8,)), pltpu.SemaphoreType.DMA((12,))],
        compiler_params=pltpu.CompilerParams(vmem_limit_bytes=62 * 2**20),
    )(*shares, pack, *through)
    return results[:5], results[5:17], results[17:]


def norm_forward(values, gain, shift):
    center = values - jnp.mean(values, axis=-1, keepdims=True)
    inverse = lax.rsqrt(jnp.mean(center * center, axis=-1, keepdims=True) + EPSILON)
    normed = center * inverse
    return (normed * gain + shift, normed, inverse)


def norm_backward(upstream, normed, inverse, gain):
    scaled = upstream * gain
    inner = (
        scaled
        - jnp.mean(scaled, axis=-1, keepdims=True)
        - normed * jnp.mean(scaled * normed, axis=-1, keepdims=True)
    )
    return (inverse * inner, jnp.sum(upstream * normed, axis=0), jnp.sum(upstream, axis=0))


def gelu_slope(values):
    return (
        0.5 * (1.0 + lax.erf(values * SQRT_HALF))
        + values * jnp.exp(-0.5 * values * values) * INV_ROOT_TAU
    )


def weight_grad(left, right):
    return lax.dot_general(
        left, right, (((0,), (0,)), ((), ())), preferred_element_type=jnp.float32
    )


def input_grad(upstream, weight):
    return lax.dot_general(
        upstream, weight, (((1,), (1,)), ((), ())), preferred_element_type=jnp.float32
    )


def masked_scores(query_heads, key_heads, key_valid, scale):
    scores = (
        jnp.einsum("cqhd,ckhd->chqk", query_heads, key_heads, preferred_element_type=jnp.float32)
        * scale
    )
    return jnp.where(key_valid, scores, -1e30)


def column_sum(values):
    return jnp.sum(values, axis=0, dtype=jnp.float32)


def local(
    tokens,
    frame_counts,
    slot_mask,
    norm1_gain,
    norm1_bias,
    w_qkv,
    q_bias,
    v_bias,
    w_out,
    out_bias,
    norm2_gain,
    norm2_bias,
    w_up,
    up_bias,
    w_down,
    down_bias,
    norm3_gain,
    norm3_bias,
    w_align,
    align_bias,
    cot_block,
    cot_align,
):
    clip_count, frame_dev, slot_count, width = tokens.shape
    align_width = w_align.shape[1]
    head_size = width // HEADS
    scale = 1.0 / math.sqrt(head_size)
    row_count = clip_count * frame_dev * slot_count
    cycle_pos = lax.axis_index("blk")
    frame_ids = cycle_pos * frame_dev + jnp.arange(frame_dev, dtype=jnp.int32)
    own_slots = lax.dynamic_slice_in_dim(slot_mask, cycle_pos * frame_dev, frame_dev, 1)
    own_mask = (frame_ids[None, :, None] < frame_counts[:, None, None]) & (own_slots > 0)
    visible = own_mask.astype(jnp.float32).reshape(row_count, 1)
    all_frames = jnp.arange(slot_mask.shape[1], dtype=jnp.int32)
    key_valid = (all_frames[None, :, None] < frame_counts[:, None, None]) & (slot_mask > 0)
    key_valid = key_valid.reshape(clip_count, 1, 1, -1)
    inputs = tokens.reshape(row_count, width).astype(jnp.float32)
    normed_one, unit_one, inverse_one = norm_forward(inputs, norm1_gain, norm1_bias)
    normed1 = normed_one.astype(jnp.bfloat16)
    projected = jnp.dot(normed1, w_qkv, preferred_element_type=jnp.float32)
    queries = (projected[:, :width] + q_bias).astype(jnp.bfloat16)
    keys_local = projected[:, width : 2 * width].astype(jnp.bfloat16)
    values_local = (projected[:, 2 * width :] + v_bias).astype(jnp.bfloat16)
    block_shape = (clip_count, frame_dev, slot_count, width)
    heads_shape = (clip_count, -1, HEADS, head_size)
    keys_all, values_all = (
        lax.all_gather(keys_local.reshape(block_shape), "blk", axis=1, tiled=True),
        lax.all_gather(values_local.reshape(block_shape), "blk", axis=1, tiled=True),
    )
    key_heads = keys_all.reshape(heads_shape)
    value_heads = values_all.reshape(heads_shape)
    query_heads = queries.reshape(heads_shape)
    scores = masked_scores(query_heads, key_heads, key_valid, scale)
    top = jnp.max(scores, axis=-1, keepdims=True)
    expo = jnp.exp(scores - top)
    total = jnp.sum(expo, axis=-1, keepdims=True)
    probs_low = (expo / total).astype(jnp.bfloat16)
    attended = jnp.einsum(
        "chqk,ckhd->cqhd", probs_low, value_heads, preferred_element_type=jnp.float32
    )
    attended = attended.astype(jnp.bfloat16).reshape(row_count, width)
    mid = inputs + jnp.dot(attended, w_out, preferred_element_type=jnp.float32) + out_bias
    normed_two, unit_two, inverse_two = norm_forward(mid, norm2_gain, norm2_bias)
    normed2 = normed_two.astype(jnp.bfloat16)
    hidden = jnp.dot(normed2, w_up, preferred_element_type=jnp.float32) + up_bias
    active = jax.nn.gelu(hidden, approximate=False).astype(jnp.bfloat16)
    after = mid + jnp.dot(active, w_down, preferred_element_type=jnp.float32) + down_bias
    block_out = (visible * after).astype(jnp.bfloat16).reshape(block_shape)
    normed_three, unit_three, inverse_three = norm_forward(after, norm3_gain, norm3_bias)
    normed3 = normed_three.astype(jnp.bfloat16)
    target = jnp.dot(normed3, w_align, preferred_element_type=jnp.float32) + align_bias
    aligned = (
        (visible * target)
        .astype(jnp.bfloat16)
        .reshape(clip_count, frame_dev, slot_count, align_width)
    )
    back_align = (visible * cot_align.reshape(row_count, align_width).astype(jnp.float32)).astype(
        jnp.bfloat16
    )
    grad_align_bias = column_sum(back_align)
    grad_w_align = weight_grad(normed3, back_align)
    back_norm3, grad_norm3_gain, grad_norm3_bias = norm_backward(
        input_grad(back_align, w_align), unit_three, inverse_three, norm3_gain
    )
    back_after = visible * cot_block.reshape(row_count, width).astype(jnp.float32) + back_norm3
    back_down = back_after.astype(jnp.bfloat16)
    grad_down_bias = column_sum(back_down)
    grad_w_down = weight_grad(active, back_down)
    back_up = (input_grad(back_down, w_down) * gelu_slope(hidden)).astype(jnp.bfloat16)
    grad_up_bias = column_sum(back_up)
    grad_w_up = weight_grad(normed2, back_up)
    back_norm2, grad_norm2_gain, grad_norm2_bias = norm_backward(
        input_grad(back_up, w_up), unit_two, inverse_two, norm2_gain
    )
    back_mid = back_after + back_norm2
    back_out = back_mid.astype(jnp.bfloat16)
    grad_out_bias = column_sum(back_out)
    grad_w_out = weight_grad(attended, back_out)
    back_attended = input_grad(back_out, w_out).astype(jnp.bfloat16).reshape(heads_shape)
    scores = masked_scores(query_heads, key_heads, key_valid, scale)
    probs = jnp.exp(scores - top) / total
    probs_low = probs.astype(jnp.bfloat16)
    back_probs = jnp.einsum(
        "cqhd,ckhd->chqk", back_attended, value_heads, preferred_element_type=jnp.float32
    )
    spread = jnp.sum(probs * back_probs, axis=-1, keepdims=True)
    back_scores = (probs * (back_probs - spread)).astype(jnp.bfloat16)
    back_queries = (
        jnp.einsum("chqk,ckhd->cqhd", back_scores, key_heads, preferred_element_type=jnp.float32)
        * scale
    )
    back_queries = back_queries.astype(jnp.bfloat16).reshape(row_count, width)
    value_terms = jnp.einsum(
        "chqk,cqhd->ckhd", probs_low, back_attended, preferred_element_type=jnp.float32
    )
    key_terms = (
        jnp.einsum("chqk,cqhd->ckhd", back_scores, query_heads, preferred_element_type=jnp.float32)
        * scale
    )
    whole_shape = (clip_count, -1, slot_count, width)
    key_share, value_share = (
        lax.psum_scatter(
            key_terms.reshape(whole_shape).astype(jnp.bfloat16),
            "blk",
            scatter_dimension=1,
            tiled=True,
        ).astype(jnp.float32),
        lax.psum_scatter(
            value_terms.reshape(whole_shape).astype(jnp.bfloat16),
            "blk",
            scatter_dimension=1,
            tiled=True,
        ).astype(jnp.float32),
    )
    back_keys = key_share.astype(jnp.bfloat16).reshape(row_count, width)
    back_values = value_share.astype(jnp.bfloat16).reshape(row_count, width)
    grad_q_bias = column_sum(back_queries)
    grad_v_bias = column_sum(back_values)
    combined = jnp.concatenate([back_queries, back_keys, back_values], axis=1)
    grad_w_qkv = weight_grad(normed1, combined)
    back_norm1, grad_norm1_gain, grad_norm1_bias = norm_backward(
        input_grad(combined, w_qkv), unit_one, inverse_one, norm1_gain
    )
    grad_tokens = (back_mid + back_norm1).astype(jnp.bfloat16).reshape(block_shape)
    vector_total = lax.psum(
        (
            grad_norm1_gain,
            grad_norm1_bias,
            grad_q_bias,
            grad_v_bias,
            grad_out_bias,
            grad_norm2_gain,
            grad_norm2_bias,
            grad_up_bias,
            grad_down_bias,
            grad_norm3_gain,
            grad_norm3_bias,
            grad_align_bias,
        ),
        ("dp", "blk"),
    )
    row_part = (
        lax.psum_scatter(grad_w_qkv, "dp", scatter_dimension=0, tiled=True),
        lax.psum_scatter(grad_w_out, "dp", scatter_dimension=0, tiled=True),
        lax.psum_scatter(grad_w_up, "dp", scatter_dimension=0, tiled=True),
        lax.psum_scatter(grad_w_down, "dp", scatter_dimension=0, tiled=True),
        lax.psum_scatter(grad_w_align, "dp", scatter_dimension=0, tiled=True),
    )
    matrix_total = (
        lax.psum(row_part[0].astype(jnp.bfloat16), "blk").astype(jnp.float32),
        lax.psum(row_part[1].astype(jnp.bfloat16), "blk").astype(jnp.float32),
        lax.psum(row_part[2].astype(jnp.bfloat16), "blk").astype(jnp.float32),
        lax.psum(row_part[3].astype(jnp.bfloat16), "blk").astype(jnp.float32),
        lax.psum(row_part[4].astype(jnp.bfloat16), "blk").astype(jnp.float32),
    )
    return (
        block_out,
        aligned,
        grad_tokens,
        vector_total[0],
        vector_total[1],
        matrix_total[0],
        vector_total[2],
        vector_total[3],
        matrix_total[1],
        vector_total[4],
        vector_total[5],
        vector_total[6],
        matrix_total[2],
        vector_total[7],
        matrix_total[3],
        vector_total[8],
        vector_total[9],
        vector_total[10],
        matrix_total[4],
        vector_total[11],
    )


def local_kernels(
    tokens, frame_counts, slot_mask, norm1_gain, norm1_bias, w_qkv, q_bias, v_bias, w_out, out_bias, norm2_gain,
    norm2_bias, w_up, up_bias, w_down, down_bias, norm3_gain, norm3_bias, w_align, align_bias, cot_block, cot_align,
):
    clip_count, frame_dev, slot_count, width = tokens.shape
    align = w_align.shape[1]
    piece = frame_dev * slot_count
    rows = clip_count * piece
    vectors = [
        norm1_gain, norm1_bias, q_bias, v_bias, out_bias, norm2_gain, norm2_bias, down_bias, norm3_gain, norm3_bias,
        up_bias, align_bias,
    ]
    block_out, align_out, grad_tokens, vec, *shares = layer(
        slot_mask, frame_counts, vectors, tokens.reshape(clip_count, piece, width), cot_align.reshape(rows, align),
        cot_block.reshape(rows, width), w_align, w_down, w_up, w_out, w_qkv,
    )
    matrices, totals, (block_out, align_out, grad_tokens) = finish(
        shares, vec, (block_out, align_out, grad_tokens), [vector.shape[0] for vector in vectors]
    )
    (
        grad_norm1_gain, grad_norm1_bias, grad_q_bias, grad_v_bias, grad_out_bias, grad_norm2_gain, grad_norm2_bias,
        grad_down_bias, grad_norm3_gain, grad_norm3_bias, grad_up_bias, grad_align_bias,
    ) = totals
    return (
        block_out.reshape(tokens.shape),
        align_out.reshape(cot_align.shape),
        grad_tokens.reshape(tokens.shape),
        grad_norm1_gain,
        grad_norm1_bias,
        matrices[0],
        grad_q_bias,
        grad_v_bias,
        matrices[1],
        grad_out_bias,
        grad_norm2_gain,
        grad_norm2_bias,
        matrices[2],
        grad_up_bias,
        matrices[3],
        grad_down_bias,
        grad_norm3_gain,
        grad_norm3_bias,
        matrices[4],
        grad_align_bias,
    )


def solution(mesh):
    in_specs = (
        P("dp", "blk", None, None),
        P("dp"),
        P("dp", None, None),
        P(),
        P(),
        P(),
        P(),
        P(),
        P(),
        P(),
        P(),
        P(),
        P(),
        P(),
        P(),
        P(),
        P(),
        P(),
        P(),
        P(),
        P("dp", "blk", None, None),
        P("dp", "blk", None, None),
    )
    out_specs = (
        P("dp", "blk", None, None),
        P("dp", "blk", None, None),
        P("dp", "blk", None, None),
        P(),
        P(),
        P("dp", None),
        P(),
        P(),
        P("dp", None),
        P(),
        P(),
        P(),
        P("dp", None),
        P(),
        P("dp", None),
        P(),
        P(),
        P(),
        P("dp", None),
        P(),
    )
    sizes = (mesh.shape["dp"], mesh.shape["blk"])
    run = local_kernels if sizes == GRID else local
    return jax.shard_map(run, mesh=mesh, in_specs=in_specs, out_specs=out_specs, check_vma=False)
```

profile of v0, /device:TPU:0, one launch (start us, length us, event | category | flops | bytes accessed | tf_op | source)
XLA Modules:
  0.0 173.1 jit_solution(5595962549483205095)
XLA Ops:
  0.7 168.4 %layer.1 = (bf16[2,4,48,768]{3,2,1,0:T(8,128)(2,1)}, bf16[2,4,48,1024]{3,2,1,0:T(8,128)(2,1)}, bf16[384,768]{1,0:T(8,128)(2,1)}, f32[16,768]{1,0:T(8,128)}, bf16...) custom-call(s32[2,16,48]{2,1,0:T(8,128)} %refs_0_.1, ...), custom_call_target="tpu_custom_call" | custom-call | tf_op jit(solution)/shard_map/layer/pallas_call | solution.py:990
  169.1 3.9 %finish.1 = (f32[96,2304]{1,0:T(8,128)}, f32[96,768]{1,0:T(8,128)}, f32[96,3072]{1,0:T(8,128)}, f32[384,768]{1,0:T(8,128)}, f32[96,1024]{1,0:T(8,128)}, /*index=...) custom-call(bf16[96,2304]{1,0:T(8,128)(2,1)} %get-tuple-element.49.r, ...), custom_call_target="tpu_custom_call" | custom-call | tf_op jit(solution)/shard_map/finish/pallas_call | solution.py:1061
where the time goes:
time: 173 us
  Pallas kernels  172 us (99%)
    pallas_call x1, Pallas kernels, layer(): pl.pallas_call(layer_kernel, name='layer', out_shape=[struct((2, 4, 48, w...  168 us
    pallas_call x1, Pallas kernels, finish(): pl.pallas_call(finish_kernel, name='finish', out_shape=[struct(share.shap...  3.91 us

commit v1 on v0

--- a/solution.py
+++ b/solution.py
@@ -92,19 +92,19 @@
 KEY_BLOCK = 256
 NORM_ROWS = 96
 PLAN = (
-    (0, "far"), (0, 0), "e3", "norm3", (0, "own"), (0, 1), (1, "far"), (1, 0), "feed", (1, "own"), (1, 1),
-    (5, "far"), (5, 0), "e2", (0, 2), "norm2", (1, 2), "back_att", (5, "own"), (5, 1), (0, 3), (2, "far"), (2, 0),
-    (2, "own"), (1, 3), (3, "far"), (3, 0), (3, "own"), (4, "far"), (4, 0), (2, 1), (6, "far"), (6, 0), (4, "own"),
-    (5, 2), (6, "own"), "settle0", (3, 1), "pair", (2, 2), "pair", (5, 3), (4, 1), "pair", (3, 2), "settle1",
-    (0, 4), (2, 3), "pair", (6, 1), "pair", (4, 2), (1, 4), (3, 3), "settle2", (5, 4), (0, 5), "pair", (6, 2),
-    "pair", (2, 4), (4, 3), (1, 5), "pair", (6, 3), (0, 6), (3, 4), (5, 5), "pair", "dx0", (4, 4), (1, 6), (2, 5),
-    (10, "far"), (10, 0), "dx1", "dx2", (11, "far"), (11, 0), (6, 4), (5, 6), (3, 5), (7, "far"), (7, 0),
-    (9, "far"), (9, 0), (11, "own"), (7, "own"), "dx3", (2, 6), (4, 5), (10, "own"), (10, 1), (9, "own"),
-    (8, "far"), (8, 0), "sums", "vec0", (11, 1), "fwd0", (8, "own"), (6, 5), (10, 2), (7, 1), (12, "far"), (12, 0),
-    "vec1", (11, 2), (10, 3), "vec2", (9, 1), "fwd1", (3, 6), (7, 2), (11, 3), "vec3", (8, 1), (4, 6), "vec4",
-    (9, 2), (7, 3), "vec5", (10, 4), (11, 4), (8, 2), "norm1", (9, 3), (12, "own"), (12, 1), (7, 4), (10, 5),
-    (6, 6), (8, 3), (12, 2), (11, 5), (9, 4), (10, 6), (12, 3), (7, 5), (8, 4), (11, 6), (12, 4), (9, 5), (7, 6),
-    (8, 5), (9, 6), (12, 5), (8, 6), (12, 6),
+    (0, "far"), (0, 0), "e3", "norm3", (2, "far"), (2, 0), (0, "own"), (0, 1), (2, "own"), (3, "far"), (3, 0),
+    "feed", (2, 1), (3, "own"), (3, 1), "e2", "norm2", "back_att", (0, 2), (6, "far"), (6, 0), (1, "far"), (1, 0),
+    (4, "own"), (2, 2), (6, "own"), (4, "far"), (4, 0), (3, 2), (1, "own"), (7, "far"), (7, 0), (7, "own"), (1, 1),
+    (5, "own"), (0, 3), (6, 1), "settle0", (5, "far"), (5, 0), (3, 3), "pair", (4, 1), "pair", "pair", (6, 2),
+    (1, 2), (0, 4), (2, 3), "settle1", (4, 2), (5, 1), "pair", (6, 3), (3, 4), "pair", (2, 4), (0, 5), "settle2",
+    (4, 3), "pair", (3, 5), (1, 3), (5, 2), "pair", (6, 4), (2, 5), "pair", (5, 3), (7, 1), (4, 4), "pair", (6, 5),
+    "dx0", (5, 4), (11, "far"), (11, 0), (8, "own"), (4, 5), (7, 2), (10, "own"), (11, "own"), (1, 4), (10, "far"),
+    (10, 0), (11, 1), (9, "far"), (9, 0), (3, 6), (5, 5), "fwd0", (7, 3), (10, 1), (9, "own"), (2, 6), (8, "far"),
+    (8, 0), (11, 2), "dx1", (1, 5), (10, 2), (11, 3), (7, 4), (9, 1), (12, "far"), (12, 0), "fwd1", "dx2", "dx3",
+    (10, 3), (9, 2), (11, 4), (8, 1), (7, 5), (4, 6), (12, "own"), "sums", (12, 1), "vec0", (10, 4), "vec1", (9, 3),
+    (8, 2), (11, 5), (9, 4), (6, 6), (8, 3), (10, 5), (12, 2), (5, 6), (8, 4), (9, 5), (12, 3), "vec2", (12, 4),
+    "norm1", (8, 5), "vec3", (12, 5), (11, 6), "vec4", (7, 6), (9, 6), (0, 6), "vec5", (10, 6), (8, 6), (1, 6),
+    (12, 6),
 )
 
 
@@ -142,7 +142,7 @@
         pack, side_v,
         align_v, down_v, up_v, out_v, low_v, tok, xall, n1, qkv, own_att, att, lse_rows, spread_rows,
         mid_v, e_v, normed, ring, slope, ld, l2, l3, la, unit2, unit3, cot_a, cot_b,
-        grad_att, n1s, grad_q,
+        grad_att, n1s,
         load_sem, send0, recv0, send1, recv1, send2, recv2, sendz, recvz, sendq, recvq, out_sem, outq_sem, vsend, vrecv,
         tok_send, tok_recv, att_send, att_recv, in_send, in_recv,
         pair_send, pair_recv, end_send, end_recv, out_send, out_recv, put_sem, vector_sem,
@@ -165,7 +165,7 @@
     is_end = (z == 0) | (z == 3)
     near, far = 3 - z, lax.rem(z + 2, 4)
     other_mid = 2 - clip
-    piece, width = tok.shape[1], tok.shape[2]
+    piece, width = tok.shape
     rows, half, wide = 2 * piece, width // 2, up_v.shape[1]
     low = jnp.bfloat16
     low_d, low_o = n1.at[pl.ds(0, rows)], n1.at[pl.ds(rows, rows)]
@@ -182,7 +182,7 @@
     def slot_rows(slot):
         return pl.ds(pl.multiple_of(slot * piece, piece), piece)
 
-    loads = {"tok": (tok_h, tok)}
+    loads = {"mine": (tok_h.at[clip], xall.at[z]), "tok": (tok_h.at[1 - clip], tok)}
     for m in range(3):
         column = pl.multiple_of(m * width + side * half, 128)
         loads["low%d" % m] = (w_qkv.at[:, pl.ds(column, half)], low_v.at[m])
@@ -195,7 +195,7 @@
     loads = {
         name: pltpu.make_async_copy(src, dst, load_sem.at[k]) for k, (name, (src, dst)) in enumerate(loads.items())
     }
-    early = ("tok", "low0", "low1", "low2")
+    early = ("mine", "tok", "low0", "low1", "low2")
     for name in early:
         loads[name].start()
     small = [pltpu.make_async_copy(src, dst, vector_sem.at[k]) for k, (src, dst) in enumerate(zip(vectors_h, vectors))]
@@ -226,8 +226,7 @@
         copy.wait()
     fill_pack(pack, VECTORS, vectors)
     vec_out[...] = jnp.zeros_like(vec_out)
-    ready("tok")
-    xall[z] = tok[clip]
+    ready("mine", "tok")
     e_v[0:128, :] = jnp.zeros((128, width), jnp.float32)
     for c in range(2):
         e_v[c : c + 1, :] = jnp.concatenate(
@@ -237,11 +236,11 @@
             ],
             axis=1,
         )
-    grad_q[...] = e_v[0:128, :].T
+    side_v[...] = e_v[0:128, :].T
+    seen = [side_v[slot_rows(z), c : c + 1] for c in range(2)]
+    side_v[:, KEY : KEY + 1] = jnp.where(jnp.where(clip == 0, side_v[:, 0:1], side_v[:, 1:2]) > 0.0, 0.0, -1e30)
     for c in range(2):
-        side_v[pl.ds(c * piece, piece), VIS : VIS + 1] = grad_q[pl.ds(pl.multiple_of(z * piece, piece), piece), c : c + 1]
-    seen = jnp.where(clip == 0, grad_q[:, 0:1], grad_q[:, 1:2])
-    side_v[:, KEY : KEY + 1] = jnp.where(seen > 0.0, 0.0, -1e30)
+        side_v[pl.ds(c * piece, piece), VIS : VIS + 1] = seen[c]
     row_bias = jnp.where(jnp.where(clip == 0, e_v[0:1, :], e_v[1:2, :]) > 0.0, 0.0, -1e30)
     columns = pl.ds(pl.multiple_of(side * half, 128), half)
     ready("low0", "low1", "low2")
@@ -261,11 +260,18 @@
         qkv[1, where, :] = dot(left, low_v[1]).astype(low)
         qkv[2, where, :] = (dot(left, low_v[2]) + pack[V_BIAS : V_BIAS + 1, columns]).astype(low)
 
+    last = 3 * (1 - clip)
+    third = 2 - clip
+    early_keys = pl.ds(pl.multiple_of(clip * piece, piece), 3 * piece)
+    late_keys = slot_rows(last)
+    early_bias = jnp.where(clip == 0, row_bias[:, : 3 * piece], row_bias[:, piece:])
+    late_bias = jnp.where(clip == 0, row_bias[:, 3 * piece :], row_bias[:, :piece])
+
+    def slot_of(number):
+        return jnp.where(number == 0, z, jnp.where(number == 1, partner, jnp.where(number == 2, third, last)))
+
     def tokens_of(number, _):
-        first, second = jnp.where(is_mid, near, far), jnp.where(is_mid, far, near)
-        slot = jnp.where(
-            number == 0, z, jnp.where(number == 1, partner, jnp.where(number == 2, first, second))
-        )
+        slot = slot_of(number)
 
         @pl.when(number == 1)
         def _():
@@ -290,45 +296,102 @@
         project(slot)
         return 0
 
-    lax.fori_loop(0, 4, tokens_of, 0)
     lane = lax.broadcasted_iota(jnp.int32, (1, 128), 1)
     low_lane = lane < 64
 
-    def att_copy(slot):
+    def att_copy(slot, t):
         return remote_copy(
-            own_att.at[slot_rows(slot)], att.at[clip, side], att_send.at[slot], att_recv.at[z], (dp, slot)
+            own_att.at[t, slot_rows(slot)], att.at[clip, side, t], att_send.at[slot, t], att_recv.at[z, t], (dp, slot)
         )
 
-    def attend(number, _):
-        slot = jnp.where(number == 0, far, jnp.where(number == 1, near, jnp.where(number == 2, partner, z)))
+    def held(number, t):
+        rows_at = pl.ds(pl.multiple_of(lax.rem(number, 2) * piece, piece), piece)
+        return rows_at, pl.ds(pl.multiple_of(number // 2 * half + t * 128, 128), 128)
+
+    def head(queries, a, keys, bias):
+        mine = low_lane if a == 0 else jnp.logical_not(low_lane)
+        return dot(jnp.where(mine, queries, jnp.zeros_like(queries)), keys, NT) + bias
+
+    def attend_early(number, _):
+        where = slot_rows(slot_of(number))
+        stats = jnp.zeros((piece, 128), jnp.float32)
+        for t in range(half // 128):
+            at = pl.ds(t * 128, 128)
+            parts = []
+            for a in range(2):
+                scores = head(qkv[0, where, at], a, qkv[1, early_keys, at], early_bias)
+                top = jnp.max(scores, axis=-1, keepdims=True)
+                expo = jnp.exp(scores - top)
+                parts.append(dot(expo.astype(low), qkv[2, early_keys, at]))
+                stats = jnp.where(lane == STATS + 2 * t + a, top, stats)
+                stats = jnp.where(lane == STATS + 8 + 2 * t + a, jnp.sum(expo, axis=-1, keepdims=True), stats)
+            e_v[held(number, t)] = jnp.where(low_lane, parts[0], parts[1])
+        side_v[where, STATS : STATS + 16] = stats[:, STATS : STATS + 16]
+        return 0
+
+    def attend_whole(slot):
         where = slot_rows(slot)
         stats = jnp.zeros((piece, 128), jnp.float32)
         for t in range(half // 128):
             at = pl.ds(t * 128, 128)
-            queries = qkv[0, where, at]
-            keys = qkv[1, :, at]
-            values = qkv[2, :, at]
             parts = []
             for a in range(2):
-                mine = low_lane if a == 0 else jnp.logical_not(low_lane)
-                masked = jnp.where(mine, queries, jnp.zeros_like(queries))
-                scores = dot(masked, keys, NT) + row_bias
+                scores = head(qkv[0, where, at], a, qkv[1, :, at], row_bias)
                 top = jnp.max(scores, axis=-1, keepdims=True)
                 expo = jnp.exp(scores - top)
                 denominator = jnp.sum(expo, axis=-1, keepdims=True)
-                parts.append(dot(expo.astype(low), values) * (1.0 / denominator))
+                parts.append(dot(expo.astype(low), qkv[2, :, at]) * (1.0 / denominator))
                 stats = jnp.where(lane == STATS + 2 * t + a, top + jnp.log(denominator), stats)
-            own_att[where, at] = jnp.where(low_lane, parts[0], parts[1]).astype(low)
+            own_att[t, where, :] = jnp.where(low_lane, parts[0], parts[1]).astype(low)
+
+            @pl.when(slot != z)
+            def _():
+                att_copy(slot, t).start()
+
         side_v[where, STATS : STATS + 8] = stats[:, STATS : STATS + 8]
 
-        @pl.when(number < 3)
-        def _():
-            att_copy(slot).start()
-
+    def attend_late(step_number, _):
+        number = 2 - step_number
+        slot = slot_of(number)
+        where = slot_rows(slot)
+        before = side_v[where, :]
+        stats = jnp.zeros((piece, 128), jnp.float32)
+        for t in range(half // 128):
+            at = pl.ds(t * 128, 128)
+            sums = e_v[held(number, t)]
+            parts = []
+            for a in range(2):
+                k = STATS + 2 * t + a
+                scores = head(qkv[0, where, at], a, qkv[1, late_keys, at], late_bias)
+                old = before[:, k : k + 1]
+                top = jnp.maximum(old, jnp.max(scores, axis=-1, keepdims=True))
+                expo = jnp.exp(scores - top)
+                kept = jnp.exp(old - top)
+                denominator = before[:, k + 8 : k + 9] * kept + jnp.sum(expo, axis=-1, keepdims=True)
+                value = sums * kept + dot(expo.astype(low), qkv[2, late_keys, at])
+                parts.append(value * (1.0 / denominator))
+                stats = jnp.where(lane == k, top + jnp.log(denominator), stats)
+            own_att[t, where, :] = jnp.where(low_lane, parts[0], parts[1]).astype(low)
+
+            @pl.when(number > 0)
+            def _():
+                att_copy(slot, t).start()
+
+        side_v[where, STATS : STATS + 8] = stats[:, STATS : STATS + 8]
         return 0
 
+    lax.fori_loop(0, 3, tokens_of, 0)
+
+    tokens_of(3, 0)
+
+    def attend(number, _):
+        attend_whole(slot_of(3 - number))
+
+        return 0
+
     lax.fori_loop(0, 4, attend, 0)
-    att[clip, side] = own_att[slot_rows(z), :]
+
+    att[clip, side] = own_att[:, slot_rows(z), :]
 
     def tiles(count, size, body):
         def one_tile(t, _):
@@ -380,11 +443,12 @@
 
     def settle_att(number, _):
         slot = lax.rem(z + number, 4)
-        att_copy(slot).wait_send()
-        remote_copy(
-            own_att.at[slot_rows(slot)], att.at[slot // 2, lax.rem(slot, 2)],
-            att_send.at[slot], att_recv.at[slot], (dp, slot),
-        ).wait_recv()
+        for t in range(half // 128):
+            att_copy(slot, t).wait_send()
+            remote_copy(
+                own_att.at[t, slot_rows(slot)], att.at[slot // 2, lax.rem(slot, 2), t],
+                att_send.at[slot, t], att_recv.at[slot, t], (dp, slot),
+            ).wait_recv()
         return 0
 
     lax.fori_loop(1, 4, settle_att, 0)
@@ -400,14 +464,17 @@
 
     for c in range(2):
         for h in range(2):
-            normed[pl.ds(c * piece, piece), pl.ds(h * half, half)] = att[c, h]
+            for t in range(half // 128):
+                normed[pl.ds(c * piece, piece), pl.ds(h * half + t * 128, 128)] = att[c, h, t]
     shares_of(normed, la, width // 8)
     ready("out")
 
     def mix(t, at):
         mixed = dot(normed[...], out_v[:, at]) + pack[OUT_BIAS : OUT_BIAS + 1, at]
-        mid_v[pl.ds(0, piece), at] = tok[0, :, at].astype(jnp.float32) + mixed[:piece]
-        mid_v[pl.ds(piece, piece), at] = tok[1, :, at].astype(jnp.float32) + mixed[piece:]
+        for c in range(2):
+            mixed_c = mixed[c * piece : (c + 1) * piece]
+            source = jnp.where(clip == c, xall[z, :, at], tok[:, at])
+            mid_v[pl.ds(c * piece, piece), at] = source.astype(jnp.float32) + mixed_c
 
     tiles(3, 256, mix)
 
@@ -464,14 +531,14 @@
     shares_of(normed, l3, width // 8)
     ready("align", "cot_b")
 
-    def head(t, at):
+    def align_tile(t, at):
         bias = pack[pl.ds(ALIGN_BIAS + t // 3, 1), pl.ds(pl.multiple_of(lax.rem(t, 3) * 256, 256), 256)]
         value = dot(normed[...], align_v[:, at]) + bias
         value = (side_v[pl.ds(0, rows), VIS : VIS + 1] * value).astype(low)
         for k in range(8):
             own[0][k // 4, k % 4, :, at] = value[k * 48 : (k + 1) * 48]
 
-    tiles(4, 256, head)
+    tiles(4, 256, align_tile)
     staged(0, align_out).start()
 
     def buffer_of(j):
@@ -741,9 +808,8 @@
         norm_pass(unit2, INV2, N2_GAIN, lambda at: mid_v[at, :], low_o, (N2_GAIN, N2_BIAS, OUT_BIAS))
 
     def in_copy(slot, t):
-        at = pl.ds(t * 128, 128)
         return remote_copy(
-            in_src.at[slot // 2, lax.rem(slot, 2), :, at], grad_att.at[z, :, at],
+            in_src.at[slot // 2, lax.rem(slot, 2), t], grad_att.at[t, z],
             in_send.at[slot, t], in_recv.at[z, t], (dp, slot),
         )
 
@@ -751,7 +817,8 @@
         for h in range(2):
             value = dot(low_o[...], out_v[pl.ds(h * half, half), :], NT).astype(low)
             for c in range(2):
-                in_src[c, h] = value[c * piece : (c + 1) * piece]
+                for t in range(half // 128):
+                    in_src[c, h, t] = value[c * piece : (c + 1) * piece, t * 128 : (t + 1) * 128]
         for t in range(half // 128):
 
             def start(number, _):
@@ -759,16 +826,15 @@
                 return 0
 
             lax.fori_loop(1, 4, start, 0)
-        grad_att[z] = in_src[clip, side]
+        for t in range(half // 128):
+            grad_att[t, z] = in_src[clip, side, t]
 
     def settle(t):
-        at = pl.ds(t * 128, 128)
-
         def body(number, _):
             slot = lax.rem(z + number, 4)
             in_copy(slot, t).wait_send()
             remote_copy(
-                in_src.at[0, 0, :, at], grad_att.at[slot, :, at], in_send.at[slot, t], in_recv.at[slot, t], (dp, slot)
+                in_src.at[0, 0, t], grad_att.at[t, slot], in_send.at[slot, t], in_recv.at[slot, t], (dp, slot)
             ).wait_recv()
             return 0
 
@@ -777,7 +843,7 @@
         def spread(slot, _):
             where = slot_rows(slot)
             stats = jnp.zeros((piece, 128), jnp.float32)
-            product = grad_att[slot, :, at].astype(jnp.float32) * own_att[where, at].astype(jnp.float32)
+            product = grad_att[t, slot].astype(jnp.float32) * own_att[t, where, :].astype(jnp.float32)
             for a in range(2):
                 mine = low_lane if a == 0 else jnp.logical_not(low_lane)
                 value = jnp.sum(jnp.where(mine, product, 0.0), axis=-1, keepdims=True)
@@ -792,13 +858,14 @@
         t, b = number // 3, lax.rem(number, 3)
         at = pl.ds(pl.multiple_of(t * 128, 128), 128)
         queries = qkv[0, :, at]
-        grads = grad_att[:, :, at].reshape(4 * piece, 128)
+        grads = grad_att[t].reshape(4 * piece, 128)
         keys_at = pl.ds(pl.multiple_of(b * KEY_BLOCK, KEY_BLOCK), KEY_BLOCK)
         keys = qkv[1, keys_at, at]
         values = qkv[2, keys_at, at]
         grad_k = jnp.zeros((KEY_BLOCK, 128), jnp.float32)
         grad_v = jnp.zeros((KEY_BLOCK, 128), jnp.float32)
-        grad_queries = jnp.where(b == 0, 0.0, grad_q[...])
+        held_q = (e_v.at[:, pl.ds(0, 128)], e_v.at[:, pl.ds(128, 128)])
+        grad_queries = jnp.where(b == 0, 0.0, jnp.concatenate([ref[...] for ref in held_q], axis=0))
         for a in range(2):
             mine = low_lane if a == 0 else jnp.logical_not(low_lane)
             zero = jnp.zeros((), low)
@@ -814,11 +881,13 @@
             grad_queries = grad_queries + dot(back, k_mine, TN)
         grad_at(1)[keys_at, at] = grad_k.astype(low)
         grad_at(2)[keys_at, at] = grad_v.astype(low)
-        grad_q[...] = grad_queries
+        for k, ref in enumerate(held_q):
+            ref[...] = grad_queries[k * rows : (k + 1) * rows]
 
         @pl.when(b == 2)
         def _():
-            grad_at(0)[:, at] = (grad_q[...] * 0.125).astype(low)
+            for k, ref in enumerate(held_q):
+                grad_at(0)[pl.ds(k * rows, rows), at] = (ref[...] * 0.125).astype(low)
 
     def pair_copy():
         return remote_copy(e_at(partner), from_pair, pair_send, pair_recv, to_z1)
@@ -886,7 +955,8 @@
 
         def body(at, k, _):
             half_clip = pl.ds(pl.multiple_of(lax.rem(k, 2) * NORM_ROWS, NORM_ROWS), NORM_ROWS)
-            one, inverse = norm_rows(tok[k // 2, half_clip, :].astype(jnp.float32))
+            source = jnp.where(clip == k // 2, xall[z, half_clip, :], tok[half_clip, :])
+            one, inverse = norm_rows(source.astype(jnp.float32))
             value = mid_v[at, :] + norm_back(e_v[at, :], one, inverse, pack[N1_GAIN : N1_GAIN + 1, :])
             low_d[at, :] = value.astype(low)
             return 0
@@ -963,24 +1033,23 @@
         + [v(vector.shape, full) for vector in vectors]
         + [v((PACK_ROWS, width), full), v((4 * piece, 128), full)]
         + [v(w_align.shape, low), v(w_down.shape, low), v(w_up.shape, low), v(w_out.shape, low)]
-        + [v((3, width, half), low), v((2, piece, width), low), v((4, piece, width), low), v((4 * piece, width), low)]
-        + [v((3, 4 * piece, half), low), v((4 * piece, half), low), v((2, 2, piece, half), low)]
+        + [v((3, width, half), low), v((piece, width), low), v((4, piece, width), low), v((4 * piece, width), low)]
+        + [v((3, 4 * piece, half), low), v((3, 4 * piece, 128), low), v((2, 2, 3, piece, 128), low)]
         + [v((8, 4 * piece), full)] * 2
         + [v((rows, width), full), v((rows, width), full), v((rows, width), low), v((8, 48, wide), low)]
         + [v((rows, wide), low), v((2, 4, wide // 8, rows), low)]
         + [v((2, 4, width // 8, rows), low)] * 3
         + [v((rows, width), low)] * 2
         + [v((rows, align), low), v((rows, width), low)]
-        + [v((4, piece, half), low), v((2, 4, width // 8, 4 * piece), low), v((4 * piece, 128), full)]
-        + [dma((10,))]
+        + [v((3, 4, piece, 128), low), v((2, 4, width // 8, 4 * piece), low)]
+        + [dma((11,))]
         + [dma((COUNT, 2))] * 6
         + [dma((PLAIN, 2, 2))] * 2
         + [dma((3, 3, 2))] * 2
         + [dma((PLAIN, 2)), dma((3, 2, 2))]
         + [dma((5,))] * 2
         + [dma((4, CHUNKS))] * 2
-        + [dma((4,))] * 2
-        + [dma((4, 3))] * 2
+        + [dma((4, 3))] * 4
         + [dma(())] * 2
         + [dma((2,))] * 2
         + [dma((2,)), dma(())]

time: 173 us -> 166 us (0.960)
  Pallas kernels: 172 us -> 165 us
    pallas_call x1, Pallas kernels: 168 us -> 161 us  [layer(): pl.pallas_call(layer_kernel, name='layer', out_shape=[struct((2, 4, 48, w...]
where the time goes in v1:
time: 166 us
  Pallas kernels  165 us (99%)
    pallas_call x1, Pallas kernels, layer(): pl.pallas_call(layer_kernel, name='layer', out_shape=[struct((2, 4, 48, w...  161 us
    pallas_call x1, Pallas kernels, finish(): pl.pallas_call(finish_kernel, name='finish', out_shape=[struct(share.shap...  3.91 us

profile of v1, /device:TPU:0, one launch (start us, length us, event | category | flops | bytes accessed | tf_op | source)
XLA Modules:
  0.0 166.2 jit_solution(10502999996237489322)
XLA Ops:
  0.7 161.4 %layer.1 = (bf16[2,4,48,768]{3,2,1,0:T(8,128)(2,1)}, bf16[2,4,48,1024]{3,2,1,0:T(8,128)(2,1)}, bf16[384,768]{1,0:T(8,128)(2,1)}, f32[16,768]{1,0:T(8,128)}, bf16...) custom-call(s32[2,16,48]{2,1,0:T(8,128)} %refs_0_.1, ...), custom_call_target="tpu_custom_call" | custom-call | tf_op jit(solution)/shard_map/layer/pallas_call | solution.py:1059
  162.1 3.9 %finish.1 = (f32[96,2304]{1,0:T(8,128)}, f32[96,768]{1,0:T(8,128)}, f32[96,3072]{1,0:T(8,128)}, f32[384,768]{1,0:T(8,128)}, f32[96,1024]{1,0:T(8,128)}, /*index=...) custom-call(bf16[96,2304]{1,0:T(8,128)(2,1)} %get-tuple-element.49.r, ...), custom_call_target="tpu_custom_call" | custom-call | tf_op jit(solution)/shard_map/finish/pallas_call | solution.py:1130

commit v2 on v1

--- a/solution.py
+++ b/solution.py
@@ -36,18 +36,6 @@
     0, 1, 2, 3, 4, 5, 6, 7, 8, 9, 10, 14,
 )
 PACK_ROWS = 16
-TILE = 512
-
-
-def row_of(pack, row, start, size):
-    width = pack.shape[1]
-    parts = []
-    while size > 0:
-        line, column = row + start // width, start % width
-        take = min(size, width - column)
-        parts.append(pack[line : line + 1, column : column + take])
-        start, size = start + take, size - take
-    return parts[0] if len(parts) == 1 else jnp.concatenate(parts, axis=1)
 
 
 def fill_pack(pack, rows, refs):
@@ -63,13 +51,6 @@
     center = values - jnp.mean(values, axis=-1, keepdims=True)
     inverse = lax.rsqrt(jnp.mean(center * center, axis=-1, keepdims=True) + EPSILON)
     return center * inverse, inverse
-
-
-def put_visible(vis, visible_t, z):
-    piece = vis.shape[0] // 2
-    for c in range(2):
-        where = pl.ds(pl.multiple_of(z * piece, piece), piece)
-        vis[pl.ds(c * piece, piece), :] = visible_t[where, c : c + 1]
 
 
 JOBS = (
@@ -90,21 +71,21 @@
 COUNT = len(JOBS)
 PLAIN = 10
 KEY_BLOCK = 256
-NORM_ROWS = 96
+NORM_ROWS = 192
 PLAN = (
-    (0, "far"), (0, 0), "e3", "norm3", (2, "far"), (2, 0), (0, "own"), (0, 1), (2, "own"), (3, "far"), (3, 0),
-    "feed", (2, 1), (3, "own"), (3, 1), "e2", "norm2", "back_att", (0, 2), (6, "far"), (6, 0), (1, "far"), (1, 0),
-    (4, "own"), (2, 2), (6, "own"), (4, "far"), (4, 0), (3, 2), (1, "own"), (7, "far"), (7, 0), (7, "own"), (1, 1),
-    (5, "own"), (0, 3), (6, 1), "settle0", (5, "far"), (5, 0), (3, 3), "pair", (4, 1), "pair", "pair", (6, 2),
-    (1, 2), (0, 4), (2, 3), "settle1", (4, 2), (5, 1), "pair", (6, 3), (3, 4), "pair", (2, 4), (0, 5), "settle2",
-    (4, 3), "pair", (3, 5), (1, 3), (5, 2), "pair", (6, 4), (2, 5), "pair", (5, 3), (7, 1), (4, 4), "pair", (6, 5),
-    "dx0", (5, 4), (11, "far"), (11, 0), (8, "own"), (4, 5), (7, 2), (10, "own"), (11, "own"), (1, 4), (10, "far"),
-    (10, 0), (11, 1), (9, "far"), (9, 0), (3, 6), (5, 5), "fwd0", (7, 3), (10, 1), (9, "own"), (2, 6), (8, "far"),
-    (8, 0), (11, 2), "dx1", (1, 5), (10, 2), (11, 3), (7, 4), (9, 1), (12, "far"), (12, 0), "fwd1", "dx2", "dx3",
-    (10, 3), (9, 2), (11, 4), (8, 1), (7, 5), (4, 6), (12, "own"), "sums", (12, 1), "vec0", (10, 4), "vec1", (9, 3),
-    (8, 2), (11, 5), (9, 4), (6, 6), (8, 3), (10, 5), (12, 2), (5, 6), (8, 4), (9, 5), (12, 3), "vec2", (12, 4),
-    "norm1", (8, 5), "vec3", (12, 5), (11, 6), "vec4", (7, 6), (9, 6), (0, 6), "vec5", (10, 6), (8, 6), (1, 6),
-    (12, 6),
+    (0, "far"), (0, 0), "e3", "norm3", (2, "far"), (2, 0), (0, "own"), (0, 1), (2, "own"), "feed", (2, 1), "e2",
+    "norm2", "back_att", (0, 2), (1, "far"), (1, 0), (3, "own"), (2, 2), (3, "far"), (3, 0), (4, "own"), (1, "own"),
+    (4, "far"), (4, 0), (1, 1), (5, "far"), (5, 0), (6, "far"), (6, 0), (2, 3), (3, 1), (5, "own"), (6, "own"),
+    "settle0", "pair", (0, 3), (1, 2), "pair", (4, 1), "pair", "settle1", (1, 3), (2, 4), (3, 2), "pair", (5, 1),
+    (4, 2), (9, "far"), (9, 0), (0, 4), "pair", (3, 3), (2, 5), "pair", (5, 2), "settle2", (1, 4), (9, "own"),
+    (4, 3), "pair", (0, 5), (9, 1), (3, 4), (5, 3), "pair", (1, 5), "pair", "dx0", (4, 4), (6, 1), (9, 2), (3, 5),
+    (10, "far"), (10, 0), (8, "own"), (8, "far"), (8, 0), "dx1", (5, 4), (10, "own"), (4, 5), (11, "far"), (11, 0),
+    (10, 1), (7, "far"), (7, 0), "fwd0", (7, "own"), (5, 5), (10, 2), (0, 6), (7, 1), (11, "own"), (2, 6), (9, 3),
+    (12, "far"), (12, 0), (11, 1), "fwd1", (10, 3), (8, 1), "dx2", "dx3", (12, "own"), (9, 4), (11, 2), "sums",
+    (10, 4), (7, 2), "vec0", (3, 6), (12, 1), (1, 6), (8, 2), (11, 3), (4, 6), (6, 2), (9, 5), (12, 2), "vec1",
+    (11, 4), (7, 3), (10, 5), (7, 4), (11, 5), (5, 6), "vec2", (8, 3), (6, 3), (9, 6), (8, 4), (7, 5), (12, 3),
+    (10, 6), (7, 6), (6, 4), (8, 5), (12, 4), (6, 5), "vec3", (8, 6), (11, 6), (12, 5), "norm1", "vec4", "vec5",
+    (6, 6), (12, 6),
 )
 
 
@@ -262,11 +243,6 @@
 
     last = 3 * (1 - clip)
     third = 2 - clip
-    early_keys = pl.ds(pl.multiple_of(clip * piece, piece), 3 * piece)
-    late_keys = slot_rows(last)
-    early_bias = jnp.where(clip == 0, row_bias[:, : 3 * piece], row_bias[:, piece:])
-    late_bias = jnp.where(clip == 0, row_bias[:, 3 * piece :], row_bias[:, :piece])
-
     def slot_of(number):
         return jnp.where(number == 0, z, jnp.where(number == 1, partner, jnp.where(number == 2, third, last)))
 
@@ -304,30 +280,9 @@
             own_att.at[t, slot_rows(slot)], att.at[clip, side, t], att_send.at[slot, t], att_recv.at[z, t], (dp, slot)
         )
 
-    def held(number, t):
-        rows_at = pl.ds(pl.multiple_of(lax.rem(number, 2) * piece, piece), piece)
-        return rows_at, pl.ds(pl.multiple_of(number // 2 * half + t * 128, 128), 128)
-
     def head(queries, a, keys, bias):
         mine = low_lane if a == 0 else jnp.logical_not(low_lane)
         return dot(jnp.where(mine, queries, jnp.zeros_like(queries)), keys, NT) + bias
-
-    def attend_early(number, _):
-        where = slot_rows(slot_of(number))
-        stats = jnp.zeros((piece, 128), jnp.float32)
-        for t in range(half // 128):
-            at = pl.ds(t * 128, 128)
-            parts = []
-            for a in range(2):
-                scores = head(qkv[0, where, at], a, qkv[1, early_keys, at], early_bias)
-                top = jnp.max(scores, axis=-1, keepdims=True)
-                expo = jnp.exp(scores - top)
-                parts.append(dot(expo.astype(low), qkv[2, early_keys, at]))
-                stats = jnp.where(lane == STATS + 2 * t + a, top, stats)
-                stats = jnp.where(lane == STATS + 8 + 2 * t + a, jnp.sum(expo, axis=-1, keepdims=True), stats)
-            e_v[held(number, t)] = jnp.where(low_lane, parts[0], parts[1])
-        side_v[where, STATS : STATS + 16] = stats[:, STATS : STATS + 16]
-        return 0
 
     def attend_whole(slot):
         where = slot_rows(slot)
@@ -350,38 +305,7 @@
 
         side_v[where, STATS : STATS + 8] = stats[:, STATS : STATS + 8]
 
-    def attend_late(step_number, _):
-        number = 2 - step_number
-        slot = slot_of(number)
-        where = slot_rows(slot)
-        before = side_v[where, :]
-        stats = jnp.zeros((piece, 128), jnp.float32)
-        for t in range(half // 128):
-            at = pl.ds(t * 128, 128)
-            sums = e_v[held(number, t)]
-            parts = []
-            for a in range(2):
-                k = STATS + 2 * t + a
-                scores = head(qkv[0, where, at], a, qkv[1, late_keys, at], late_bias)
-                old = before[:, k : k + 1]
-                top = jnp.maximum(old, jnp.max(scores, axis=-1, keepdims=True))
-                expo = jnp.exp(scores - top)
-                kept = jnp.exp(old - top)
-                denominator = before[:, k + 8 : k + 9] * kept + jnp.sum(expo, axis=-1, keepdims=True)
-                value = sums * kept + dot(expo.astype(low), qkv[2, late_keys, at])
-                parts.append(value * (1.0 / denominator))
-                stats = jnp.where(lane == k, top + jnp.log(denominator), stats)
-            own_att[t, where, :] = jnp.where(low_lane, parts[0], parts[1]).astype(low)
-
-            @pl.when(number > 0)
-            def _():
-                att_copy(slot, t).start()
-
-        side_v[where, STATS : STATS + 8] = stats[:, STATS : STATS + 8]
-        return 0
-
     lax.fori_loop(0, 3, tokens_of, 0)
-
     tokens_of(3, 0)
 
     def attend(number, _):
@@ -596,29 +520,22 @@
             for copy in copies0(j):
                 copy.start()
         if number == 1:
-            for copy in copies0(j):
-                copy.wait()
-            add_into(own[j], own[j], got0[j])
-            for copy in copies1(j):
-                copy.start()
+            for h, (arrived, onward) in enumerate(zip(copies0(j), copies1(j))):
+                arrived.wait()
+                add_into(own[j].at[h], own[j].at[h], got0[j].at[h])
+                onward.start()
         if number == 2:
-            for copy in copies1(j):
-                copy.wait()
-            first, second = (own[j].at[0, pl.ds(2 * x, 2)], own[j].at[1, pl.ds(2 * y, 2)])
-            add_into(first, first, got1[j].at[0])
-            add_into(second, second, got1[j].at[1])
-            for copy in copies2(j):
-                copy.start()
+            for h, (arrived, onward) in enumerate(zip(copies1(j), copies2(j))):
+                arrived.wait()
+                kept = own[j].at[h, pl.ds(2 * (y if h else x), 2)]
+                add_into(kept, kept, got1[j].at[h])
+                onward.start()
         if number == 3:
-            for copy in copies2(j):
-                copy.wait()
-            for h, share in enumerate(shares(j)):
+            onward = list(copiesq(j, None, 0, to_z1) if j >= PLAIN else copiesz(j, 0, to_z1))
+            for h, (arrived, share) in enumerate(zip(copies2(j), shares(j))):
+                arrived.wait()
                 add_into(share, share, got2[j].at[h])
-
-            @pl.when(is_end)
-            def _():
-                for copy in copiesq(j, None, 0, to_z1) if j >= PLAIN else copiesz(j, 0, to_z1):
-                    copy.start()
+                pl.when(is_end)(onward[h].start)
 
         if number >= 4 and j >= PLAIN:
             stage_q(j, number)
@@ -627,12 +544,10 @@
 
             @pl.when(is_mid)
             def _():
-                for copy in copiesz(j, 0, to_z1):
-                    copy.wait_recv()
-                for h, share in enumerate(shares(j)):
-                    add_into(share, share, gotz[j].at[0, h])
-                for copy in copiesz(j, 1, to_z3):
-                    copy.start()
+                for h, (arrived, onward) in enumerate(zip(copiesz(j, 0, to_z1), copiesz(j, 1, to_z3))):
+                    arrived.wait_recv()
+                    add_into(shares(j)[h], shares(j)[h], gotz[j].at[0, h])
+                    onward.start()
 
             @pl.when(is_end)
             def _():
@@ -643,14 +558,11 @@
 
             @pl.when(is_mid)
             def _():
-                for copy in copiesz(j, 1, to_z3):
-                    copy.wait()
-                for h, share in enumerate(shares(j)):
-                    add_into(share, share, gotz[j].at[1, h])
-                for copy in copiesz(j, 0, to_z1):
-                    copy.start()
-                for h, share in enumerate(shares(j)):
-                    result(j, h, share).start()
+                for h, (arrived, onward) in enumerate(zip(copiesz(j, 1, to_z3), copiesz(j, 0, to_z1))):
+                    arrived.wait()
+                    add_into(shares(j)[h], shares(j)[h], gotz[j].at[1, h])
+                    onward.start()
+                    result(j, h, shares(j)[h]).start()
 
         if number == 6:
 
@@ -954,8 +866,7 @@
         e_v[slot_rows(1 - clip), :] = total_in[...].astype(jnp.float32)
 
         def body(at, k, _):
-            half_clip = pl.ds(pl.multiple_of(lax.rem(k, 2) * NORM_ROWS, NORM_ROWS), NORM_ROWS)
-            source = jnp.where(clip == k // 2, xall[z, half_clip, :], tok[half_clip, :])
+            source = jnp.where(clip == k, xall[z], tok[...])
             one, inverse = norm_rows(source.astype(jnp.float32))
             value = mid_v[at, :] + norm_back(e_v[at, :], one, inverse, pack[N1_GAIN : N1_GAIN + 1, :])
             low_d[at, :] = value.astype(low)

time: 166 us -> 165 us (level)
    pallas_call x1, Pallas kernels: 161 us -> 160 us  [layer(): pl.pallas_call(layer_kernel, name='layer', out_shape=[struct((2, 4, 48, w...]
where the time goes in v2:
time: 165 us; the launch traced here: 164 us
  Pallas kernels  164 us (99%)
    pallas_call x1, Pallas kernels, layer(): pl.pallas_call(layer_kernel, name='layer', out_shape=[struct((2, 4, 48, w...  160 us
    pallas_call x1, Pallas kernels, finish(): pl.pallas_call(finish_kernel, name='finish', out_shape=[struct(share.shap...  3.91 us

profile of v2, /device:TPU:0, one launch (start us, length us, event | category | flops | bytes accessed | tf_op | source)
XLA Modules:
  0.0 164.5 jit_solution(2355966947425605706)
XLA Ops:
  0.7 159.7 %layer.1 = (bf16[2,4,48,768]{3,2,1,0:T(8,128)(2,1)}, bf16[2,4,48,1024]{3,2,1,0:T(8,128)(2,1)}, bf16[384,768]{1,0:T(8,128)(2,1)}, f32[16,768]{1,0:T(8,128)}, bf16...) custom-call(s32[2,16,48]{2,1,0:T(8,128)} %refs_0_.1, ...), custom_call_target="tpu_custom_call" | custom-call | tf_op jit(solution)/shard_map/layer/pallas_call | solution.py:970
  160.4 3.9 %finish.1 = (f32[96,2304]{1,0:T(8,128)}, f32[96,768]{1,0:T(8,128)}, f32[96,3072]{1,0:T(8,128)}, f32[384,768]{1,0:T(8,128)}, f32[96,1024]{1,0:T(8,128)}, /*index=...) custom-call(bf16[96,2304]{1,0:T(8,128)(2,1)} %get-tuple-element.49.r, ...), custom_call_target="tpu_custom_call" | custom-call | tf_op jit(solution)/shard_map/finish/pallas_call | solution.py:1041

commit v3 on v2

--- a/solution.py
+++ b/solution.py
@@ -1006,9 +1006,9 @@
         for k in range(3)
     ]
     pack_in = pltpu.make_async_copy(pack, pack_v, in_sem.at[8])
+    for copy, _ in through:
+        copy.start()
     for copy in [pack_in] + ins:
-        copy.start()
-    for copy, _ in through:
         copy.start()
     width = pack.shape[1]
     vectors_out = [
@@ -1022,13 +1022,13 @@
             ref[pl.ds(start, size)] = pack_v[line : line + 1, 0:size].reshape(size)
     for copy in vectors_out:
         copy.start()
+    for first, second in through:
+        first.wait()
+        second.start()
     for k in range(5):
         ins[k].wait()
         wide_v[k][...] = low_v[k][...].astype(jnp.float32)
         outs[k].start()
-    for first, second in through:
-        first.wait()
-        second.start()
     for copy in outs + vectors_out:
         copy.wait()
     for _, copy in through:

time: 165 us -> 165 us (level)
  no operation moved by 1% of the time
where the time goes in v3:
time: 165 us
  Pallas kernels  164 us (99%)
    pallas_call x1, Pallas kernels, layer(): pl.pallas_call(layer_kernel, name='layer', out_shape=[struct((2, 4, 48, w...  160 us
    pallas_call x1, Pallas kernels, finish(): pl.pallas_call(finish_kernel, name='finish', out_shape=[struct(share.shap...  4.26 us

profile of v3, /device:TPU:0, one launch (start us, length us, event | category | flops | bytes accessed | tf_op | source)
XLA Modules:
  0.0 164.8 jit_solution(1137533110691126427)
XLA Ops:
  0.7 159.7 %layer.1 = (bf16[2,4,48,768]{3,2,1,0:T(8,128)(2,1)}, bf16[2,4,48,1024]{3,2,1,0:T(8,128)(2,1)}, bf16[384,768]{1,0:T(8,128)(2,1)}, f32[16,768]{1,0:T(8,128)}, bf16...) custom-call(s32[2,16,48]{2,1,0:T(8,128)} %refs_0_.1, ...), custom_call_target="tpu_custom_call" | custom-call | tf_op jit(solution)/shard_map/layer/pallas_call | solution.py:970
  160.4 4.3 %finish.1 = (f32[96,2304]{1,0:T(8,128)}, f32[96,768]{1,0:T(8,128)}, f32[96,3072]{1,0:T(8,128)}, f32[384,768]{1,0:T(8,128)}, f32[96,1024]{1,0:T(8,128)}, /*index=...) custom-call(bf16[96,2304]{1,0:T(8,128)(2,1)} %get-tuple-element.49.r, ...), custom_call_target="tpu_custom_call" | custom-call | tf_op jit(solution)/shard_map/finish/pallas_call | solution.py:1041
